TPU v7x, 512 devices: a whole 4x4x16 slice. The times are simulated.
512 devices in a mesh: blk: 16 (over y, x_hi, core), dom: 32 (over z, x_lo).
Axes of the slice: x: 4 (x_hi: 2, x_lo: 2; x = x_hi * 2 + x_lo), y: 4, z: 16, core: 2. Of those that a mesh axis runs over, the one named last changes fastest.
Arguments:
- hidden_values: bfloat16 [65536, 256], P(('blk', 'dom')), may hold values from -6 to 6
- node_scale: float32 [65536], P(('blk', 'dom')), may hold values from 0.25 to 2
- node_weight: int32 [65536], P(('blk', 'dom')), may hold values from 8 to 24
- weight: bfloat16 [256, 256], replicated, may hold values from -0.375 to 0.375
- cotangent: bfloat16 [65536, 256], P(('blk', 'dom')), may hold values from -6 to 6
- block_rows: int32 [16, 32, 96], P('blk', 'dom'), may hold values from 0 to 31
- block_cols: int32 [16, 32, 96], P('blk', 'dom'), may hold values from 0 to 15
- block_count: int32 [16, 32], P('blk', 'dom'), may hold values from 1 to 96, as said below
- edge_counts: bfloat16 [16, 32, 96, 128, 128], P('blk', 'dom'), may hold values from 0 to 3, as said below
Outputs:
- activated: bfloat16 [65536, 256], P(('blk', 'dom'))
- grad_hidden: bfloat16 [65536, 256], P(('blk', 'dom'))
Inputs may be any that keep to these rules, and one draw needn't show every extreme that they name: The first block_count[b, d] slots of a device hold its blocks and the others are unused; some device uses all 96 slots. `edge_counts`: whole numbers of edges; most entries of a block are zero.
All inputs are finite; a program needn't handle non-finite values.
Results may differ from a plain program's by a relative error of at most 0.028.
Values may be sent and summed in bfloat16 or wider, within the bound.
No kernel may reach another device: no remote copies, remote signals or barrier semaphores. Data moves between devices by JAX's collectives and lax.ppermute only.
A program may use at most 64 MiB of HBM per device.

v0:
```python
import jax
import jax.numpy as jnp
from jax import lax
from jax.sharding import PartitionSpec as P

HID = 256
BSZ = 128
QDEN = 192


slot_group = 16


def add_group(running, offset, edge_local, live_count, pick_index, place_index, source, pattern):
    chosen = lax.dynamic_slice_in_dim(edge_local, offset, slot_group, 0)
    slot_ids = offset + jnp.arange(slot_group, dtype=jnp.int32)
    chosen = jnp.where((slot_ids < live_count)[:, None, None], chosen, jnp.zeros_like(chosen))
    pick_rows = lax.dynamic_slice_in_dim(pick_index, offset, slot_group, 0)
    places = lax.dynamic_slice_in_dim(place_index, offset, slot_group, 0)
    tile_rows = jnp.take(source, pick_rows, axis=0)
    contrib = jnp.einsum(pattern, chosen, tile_rows, preferred_element_type=jnp.float32)
    return running.at[places].add(contrib)


def accumulate(
    running, group_turns, edge_local, live_count, pick_index, place_index, source, pattern
):

    def one_group(group_number, current):
        return add_group(
            current,
            group_number * slot_group,
            edge_local,
            live_count,
            pick_index,
            place_index,
            source,
            pattern,
        )

    return lax.fori_loop(0, group_turns, one_group, running)


def slope_of(preact):
    sigmoid_pre = jax.nn.sigmoid(preact)
    return sigmoid_pre * (1.0 + preact * (1.0 - sigmoid_pre))


def per_device(
    hidden_values,
    node_scale,
    node_weight,
    weight,
    cotangent,
    block_rows,
    block_cols,
    block_count,
    edge_counts,
):
    own_rows = hidden_values.shape[0]
    node_norm = node_weight.astype(jnp.float32) / QDEN
    scaled = (hidden_values.astype(jnp.float32) * (node_scale * node_norm)[:, None]).astype(
        jnp.bfloat16
    )
    gathered = lax.all_gather(scaled, "blk", axis=0, tiled=True)
    column_tiles = gathered.reshape(-1, BSZ, HID)
    edge_local = edge_counts[0, 0]
    rows_local = block_rows[0, 0]
    cols_local = block_cols[0, 0]
    live_count = block_count[0, 0]
    slot_total = edge_local.shape[0]
    group_turns = slot_total // slot_group
    row_blocks = lax.axis_size("dom") * (own_rows // BSZ)
    forward_sums = accumulate(
        jnp.zeros((row_blocks, BSZ, HID), jnp.float32),
        group_turns,
        edge_local,
        live_count,
        cols_local,
        rows_local,
        column_tiles,
        "kji,kjh->kih",
    )
    forward_flat = forward_sums.reshape(row_blocks * BSZ, HID)
    summed = lax.psum_scatter(
        forward_flat.astype(jnp.bfloat16), "dom", scatter_dimension=0, tiled=True
    ).astype(jnp.float32)
    aggregated = (summed * node_norm[:, None]).astype(jnp.bfloat16)
    preact = jnp.dot(aggregated, weight, preferred_element_type=jnp.float32)
    activated = jax.nn.silu(preact).astype(jnp.bfloat16)
    dpre = (cotangent.astype(jnp.float32) * slope_of(preact)).astype(jnp.bfloat16)
    back_own = (
        jnp.dot(dpre, weight.T, preferred_element_type=jnp.float32) * node_norm[:, None]
    ).astype(jnp.bfloat16)
    back_all = lax.all_gather(back_own, "dom", axis=0, tiled=True)
    row_tiles = back_all.reshape(-1, BSZ, HID)
    column_blocks = column_tiles.shape[0]
    backward_sums = accumulate(
        jnp.zeros((column_blocks, BSZ, HID), jnp.float32),
        group_turns,
        edge_local,
        live_count,
        rows_local,
        cols_local,
        row_tiles,
        "kji,kih->kjh",
    )
    column_sums = lax.psum_scatter(
        backward_sums.reshape(column_blocks * BSZ, HID).astype(jnp.bfloat16),
        "blk",
        scatter_dimension=0,
        tiled=True,
    ).astype(jnp.float32)
    grad_hidden = (column_sums * node_norm[:, None]).astype(jnp.bfloat16)
    return (activated, grad_hidden)


def solution(mesh):
    return jax.shard_map(
        per_device,
        mesh=mesh,
        in_specs=(
            P(("blk", "dom"), None),
            P(("blk", "dom")),
            P(("blk", "dom")),
            P(),
            P(("blk", "dom"), None),
            P("blk", "dom", None),
            P("blk", "dom", None),
            P("blk", "dom"),
            P("blk", "dom", None, None, None),
        ),
        out_specs=(P(("blk", "dom"), None), P(("blk", "dom"), None)),
        check_vma=False,
    )
```

profile of v0, /device:TPU:1, one launch (start us, length us, event | category | flops | bytes accessed | tf_op | source)
XLA Modules:
  0.0 574.0 jit_solution(5993749015452363039)
XLA Ops:
  9.6 68.3 %all-gather.3.cloned.1.call-done = bf16[2048,256]{1,0:T(8,128)(2,1)} async-done(((bf16[128,256]{1,0:T(8,128)(2,1)}), bf16[2048,256]{1,0:T(8,128)(2,1)}) %all-gather.3.cloned.1.call-update) | async-done | bytes 1048592 | tf_op jit(solution)/shard_map/all_gather | solution.py:65
  77.9 2.4 broadcast_in_dim.111
  80.3 65.0 %while.26 = (s32[]{:T(128)}, f32[32,128,256]{2,1,0:T(8,128)}, s32[96]{0:T(128)S(1)}, s32[]{:T(128)}, bf16[96,128,128]{2,1,0:T(8,128)(2,1)}, /*index=5*/s32[96]{0...) while((s32[]{:T(128)}, f32[32,128,256]{2,1,0:T(8,128)}, ...), condition=%wide.region_2.3_spmd, body=%wide.region_0.2_spmd.sunk | while | flops 135529648 | bytes 14160559 | solution.py:41
  81.1 1.8 gather_fusion
  86.7 4.4 scatter_fusion
  91.9 1.8 gather_fusion
  97.5 4.5 scatter_fusion
  102.7 1.8 gather_fusion
  108.3 4.5 scatter_fusion
  113.6 1.8 gather_fusion
  119.2 4.5 scatter_fusion
  124.4 1.8 gather_fusion
  130.0 4.5 scatter_fusion
  140.8 4.6 scatter_fusion
  145.4 3.8 convert_element_type.48
  149.3 114.0 %reduce-scatter.3.cloned.1.call-done = bf16[128,256]{1,0:T(8,128)(2,1)} async-done(((bf16[4096,256]{1,0:T(8,128)(2,1)}), bf16[128,256]{1,0:T(8,128)(2,1)}) %reduce-scatter.3.cloned.1.call-update) | async-done | bytes 65552 | tf_op jit(solution)/shard_map/reduce_scatter | solution.py:85
  265.9 134.2 %all-gather.5.cloned.1.call-done = bf16[4096,256]{1,0:T(8,128)(2,1)} async-done(((bf16[128,256]{1,0:T(8,128)(2,1)}), bf16[4096,256]{1,0:T(8,128)(2,1)}) %all-gather.5.cloned.1.call-update) | async-done | bytes 2097168 | tf_op jit(solution)/shard_map/all_gather | solution.py:95
  401.7 53.9 %while.27 = (s32[]{:T(128)}, f32[16,128,256]{2,1,0:T(8,128)}, s32[96]{0:T(128)S(1)}, s32[]{:T(128)}, bf16[96,128,128]{2,1,0:T(8,128)(2,1)}, /*index=5*/s32[96]{0...) while((s32[]{:T(128)}, f32[16,128,256]{2,1,0:T(8,128)}, ...), condition=%wide.region_6.7_spmd, body=%wide.region_4.6_spmd.sunk | while | flops 135529648 | bytes 12063407 | solution.py:41
  402.4 2.2 gather_fusion.1
  406.3 4.4 scatter_fusion.1
  411.4 2.2 gather_fusion.1
  415.2 4.4 scatter_fusion.1
  420.3 2.2 gather_fusion.1
  424.2 4.5 scatter_fusion.1
  429.4 2.2 gather_fusion.1
  433.3 4.3 scatter_fusion.1
  438.3 2.2 gather_fusion.1
  442.2 4.4 scatter_fusion.1
  447.3 2.2 gather_fusion.1
  451.2 4.4 scatter_fusion.1
  455.6 2.7 convert_element_type.56
  458.3 107.6 %reduce-scatter.5.cloned.1.call-done = bf16[128,256]{1,0:T(8,128)(2,1)} async-done(((bf16[2048,256]{1,0:T(8,128)(2,1)}), bf16[128,256]{1,0:T(8,128)(2,1)}) %reduce-scatter.5.cloned.1.call-update) | async-done | bytes 65552 | tf_op jit(solution)/shard_map/reduce_scatter | solution.py:108
  (83 shorter events, 51.0 us)
Async XLA Ops:
  7.2 256.1 %copy-start = (bf16[256,256]{1,0:T(8,128)(2,1)S(1)}, bf16[256,256]{1,0:T(8,128)(2,1)}, u32[]{:S(2)}) copy-start(bf16[256,256]{1,0:T(8,128)(2,1)} %param.16) | copy-start | bytes 393220
  7.2 70.7 %all-gather.3.cloned.1.call-start = ((), (), s32[]{:S(2)}) async-start(), calls=%async_computation.2 | async-start | bytes 1114112 | tf_op jit(solution)/shard_map/all_gather | solution.py:65
  9.5 253.8 %reduce-scatter.3.cloned.1.call-start = ((), (), s32[]{:S(2)}) async-start(), calls=%async_computation.3 | async-start | bytes 2162688 | tf_op jit(solution)/shard_map/reduce_scatter | solution.py:85
  77.9 2.4 copy-start.1
  77.9 2.4 copy-start.2
  149.2 115.8 %copy-start.3 = (bf16[128,256]{1,0:T(8,128)(2,1)S(1)}, bf16[128,256]{1,0:T(8,128)(2,1)}, u32[]{:S(2)}) copy-start(bf16[128,256]{1,0:T(8,128)(2,1)} %param.17) | copy-start | bytes 196612
  149.2 250.9 %all-gather.5.cloned.1.call-start = ((), (), s32[]{:S(2)}) async-start(), calls=%async_computation.4 | async-start | bytes 2162688 | tf_op jit(solution)/shard_map/all_gather | solution.py:95
  265.9 300.0 %reduce-scatter.5.cloned.1.call-start = ((), (), s32[]{:S(2)}) async-start(), calls=%async_computation.5 | async-start | bytes 1114112 | tf_op jit(solution)/shard_map/reduce_scatter | solution.py:108
Sparse Core Ops, SparseCore 0:
  11.9 65.9 all-gather.2
  149.3 113.9 reduce-scatter.2
  266.2 133.9 all-gather.4
  458.5 107.3 reduce-scatter.4
where the time goes:
time: 577 us; the launch traced here: 574 us
  waiting for transfers between devices  424 us (73%)
  other arithmetic  73.5 us (13%)
  local copies, waits for them, and re-layouts  41.1 us (7%)
  matrix products  21 us (4%)
  between operations  13.8 us (2%)
    all_gather x1, waiting for transfers between devices, per_device(): back_all = lax.all_gather(back_own, 'dom', axis=0, tiled=True)  134 us
    reduce_scatter x1, waiting for transfers between devices, per_device(): lax.psum_scatter(forward_flat.astype(jnp.bfloat16), 'dom', scatter_dimens...  114 us
    reduce_scatter x1, waiting for transfers between devices, per_device(): lax.psum_scatter(backward_sums.reshape(column_blocks * BSZ, HID).astype(j...  108 us
    all_gather x1, waiting for transfers between devices, per_device(): gathered = lax.all_gather(scaled, 'blk', axis=0, tiled=True)  68.3 us
    scatter-add x12, other arithmetic, add_group(): return running.at[places].add(contrib)  53.4 us
    gather x12, local copies, waits for them, and re-layouts, add_group(): tile_rows = jnp.take(source, pick_rows, axis=0)  24.3 us
    dot_general x12, matrix products, add_group(): jnp.einsum(pattern, chosen, tile_rows, preferred_element_type=jnp.float32)  18.5 us
    dynamic_slice x12, local copies, waits for them, and re-layouts, add_group(): chosen = lax.dynamic_slice_in_dim(edge_local, offset, slot_group, 0)  12.8 us
  transfers between devices with their start and end apart: 4, of which 4 were waited for; matrix products, arithmetic and copies ran while one was open for 0% of the time, Pallas kernels for 0%

commit v1 on v0

v1 whole, which is shorter than its diff:
```python
import functools

import jax
import jax.numpy as jnp
from jax import lax
from jax.experimental import pallas as pl
from jax.experimental.pallas import tpu as pltpu
from jax.sharding import Mesh, PartitionSpec as P

HID = 256
BSZ = 128
QDEN = 192
GROUP = 4
CHUNK = 16

NAMES = ("y", "xh", "core", "zh", "zl", "xl")
BLK = ("y", "xh", "core")
DOM = ("zh", "zl", "xl")


def spmm_kernel(
    transposed, count_ref, src_ref, dst_ref, edges_ref, first_ref, second_ref, out_ref, edge_buf, table, acc, sems
):
    slots = edge_buf.shape[0]
    count = count_ref[0]
    half = first_ref.shape[0]
    blocks = out_ref.shape[0]
    for c in range(slots // CHUNK):

        @pl.when(c * CHUNK < count)
        def _():
            part = pl.ds(c * CHUNK, CHUNK)
            pltpu.make_async_copy(edges_ref.at[part], edge_buf.at[part], sems.at[c]).start()

    if second_ref is not None:
        table[:half] = first_ref[...]
        table[half:] = second_ref[...]
        source = table
    else:
        source = first_ref
    acc[...] = jnp.zeros_like(acc)
    contract = (((0,), (0,)), ((), ())) if transposed else (((1,), (0,)), ((), ()))

    for c in range(slots // CHUNK):

        @pl.when(c * CHUNK < count)
        def _():
            part = pl.ds(c * CHUNK, CHUNK)
            pltpu.make_async_copy(edges_ref.at[part], edge_buf.at[part], sems.at[c]).wait()

            def step(g, carry):
                base = c * CHUNK + g * GROUP
                products = []
                for u in range(GROUP):
                    k = base + u
                    products.append(
                        lax.dot_general(
                            edge_buf[k], source[src_ref[k]], contract, preferred_element_type=jnp.float32
                        )
                    )
                for u in range(GROUP):
                    k = base + u
                    place = jnp.where(k < count, dst_ref[k], blocks)
                    acc[place] += products[u]
                return carry

            lax.fori_loop(0, CHUNK // GROUP, step, 0)

    out_ref[...] = acc[:blocks].astype(jnp.bfloat16)


def spmm(transposed, count, src, dst, edges, first, second, blocks):
    slots = edges.shape[0]
    vmem = pl.BlockSpec(memory_space=pltpu.VMEM)
    smem = pl.BlockSpec(memory_space=pltpu.SMEM)
    tables = [first] if second is None else [first, second]

    def body(count_ref, src_ref, dst_ref, edges_ref, *rest):
        first_ref = rest[0]
        second_ref = None if second is None else rest[1]
        out_ref, edge_buf, table, acc, sems = rest[len(tables) :]
        spmm_kernel(
            transposed, count_ref, src_ref, dst_ref, edges_ref, first_ref, second_ref, out_ref, edge_buf, table, acc, sems
        )

    table_rows = 1 if second is None else 2 * first.shape[0]
    return pl.pallas_call(
        body,
        out_shape=jax.ShapeDtypeStruct((blocks, BSZ, HID), jnp.bfloat16),
        in_specs=[smem, smem, smem, pl.BlockSpec(memory_space=pl.ANY)] + [vmem] * len(tables),
        out_specs=vmem,
        scratch_shapes=[
            pltpu.VMEM((slots, BSZ, BSZ), jnp.bfloat16),
            pltpu.VMEM((table_rows, BSZ, HID), jnp.bfloat16),
            pltpu.VMEM((blocks + 1, BSZ, HID), jnp.float32),
            pltpu.SemaphoreType.DMA((slots // CHUNK,)),
        ],
        compiler_params=pltpu.CompilerParams(vmem_limit_bytes=32 * 1024 * 1024),
        cost_estimate=pl.CostEstimate(
            flops=2 * slots * BSZ * BSZ * HID, bytes_accessed=2 * slots * BSZ * BSZ, transcendentals=0
        ),
    )(count, src, dst, edges, *tables)


def middle_kernel(parts_ref, norm_ref, weight_ref, cotangent_ref, activated_ref, back_ref):
    total = jnp.sum(parts_ref[...].astype(jnp.float32), axis=0)
    norm = norm_ref[...]
    aggregated = (total * norm).astype(jnp.bfloat16)
    weight = weight_ref[...]
    preact = jnp.dot(aggregated, weight, preferred_element_type=jnp.float32)
    gate = jax.nn.sigmoid(preact)
    activated_ref[...] = (preact * gate).astype(jnp.bfloat16)
    slope = gate * (1.0 + preact * (1.0 - gate))
    dpre = (cotangent_ref[...].astype(jnp.float32) * slope).astype(jnp.bfloat16)
    back = lax.dot_general(dpre, weight, (((1,), (1,)), ((), ())), preferred_element_type=jnp.float32)
    back = (back * norm).astype(jnp.bfloat16)
    for i in range(back_ref.shape[0]):
        back_ref[i] = back


def middle(parts, norm, weight, cotangent, copies):
    vmem = pl.BlockSpec(memory_space=pltpu.VMEM)
    return pl.pallas_call(
        middle_kernel,
        out_shape=(
            jax.ShapeDtypeStruct(cotangent.shape, jnp.bfloat16),
            jax.ShapeDtypeStruct((copies,) + cotangent.shape, jnp.bfloat16),
        ),
        in_specs=[vmem] * 4,
        out_specs=(vmem, vmem),
    )(parts, norm, weight, cotangent)


def exchange(value, axes):
    return lax.all_to_all(value, axes, 0, 0, tiled=True)


def other_core(value):
    return lax.ppermute(value, "core", [(0, 1), (1, 0)])


def add_up(value):
    return jnp.sum(value.astype(jnp.float32), axis=0)


def per_device(
    hidden_values, node_scale, node_weight, weight, cotangent, block_rows, block_cols, block_count, edge_counts
):
    core = lax.axis_index("core")
    node_norm = node_weight.astype(jnp.float32) / QDEN
    norm = node_norm[:, None]
    scaled = (hidden_values.astype(jnp.float32) * (node_scale * node_norm)[:, None]).astype(jnp.bfloat16)
    edges = edge_counts[0, 0]
    rows = block_rows[0, 0]
    cols = block_cols[0, 0]
    count = block_count[0]
    row_at = (rows & 3) * 8 + (rows >> 2)
    col_at = ((cols & 1) ^ core) * 8 + (cols >> 1)

    mine = exchange(jnp.broadcast_to(scaled[None], (8, BSZ, HID)), ("y", "xh"))
    theirs = other_core(mine)
    partial = spmm(True, count, col_at, row_at, edges, mine, theirs, 32)
    near = exchange(partial, ("zl", "xl"))
    near = add_up(near.reshape(4, 8, BSZ, HID)).astype(jnp.bfloat16)
    far = exchange(near, ("zh",))
    activated, back = middle(far, norm, weight, cotangent, 8)

    back = exchange(back, ("zh",))
    back = exchange(jnp.broadcast_to(back[None], (4, 8, BSZ, HID)).reshape(32, BSZ, HID), ("zl", "xl"))
    partial = spmm(False, count, row_at, col_at, edges, back, None, 16)
    received = other_core(partial[8:])
    pair = (partial[:8].astype(jnp.float32) + received.astype(jnp.float32)).astype(jnp.bfloat16)
    pair = exchange(pair, ("y", "xh"))
    grad_hidden = (add_up(pair) * norm).astype(jnp.bfloat16)
    return activated, grad_hidden


def solution(mesh):
    fine = Mesh(mesh.devices.reshape(4, 2, 2, 8, 2, 2), NAMES)
    return jax.shard_map(
        per_device,
        mesh=fine,
        in_specs=(
            P(BLK + DOM, None),
            P(BLK + DOM),
            P(BLK + DOM),
            P(),
            P(BLK + DOM, None),
            P(BLK, DOM, None),
            P(BLK, DOM, None),
            P(BLK, DOM),
            P(BLK, DOM, None, None, None),
        ),
        out_specs=(P(BLK + DOM, None), P(BLK + DOM, None)),
        check_vma=False,
    )
```

time: 577 us -> 201 us (0.35)
  waiting for transfers between devices: 424 us -> 22.6 us
  blocking collectives: 0 us -> 124 us
  other arithmetic: 73.5 us -> 4.47 us
  local copies, waits for them, and re-layouts: 41.1 us -> 3.75 us
  starting transfers between devices: 0.16 us -> 29.6 us
  matrix products: 21 us -> 0 us
  Pallas kernels: 0 us -> 14.6 us
  between operations: 13.8 us -> 1.37 us
    reduce_scatter x2 -> x0, waiting for transfers between devices: 222 us -> none  [the longest x1 114 us: per_device(): lax.psum_scatter(forward_flat.astype(jnp.bfloat16), 'dom', scatter_dimens...]
    all_gather x2 -> x0, waiting for transfers between devices: 203 us -> none  [the longest x1 134 us: per_device(): back_all = lax.all_gather(back_own, 'dom', axis=0, tiled=True)]
    all_to_all x0 -> x5, blocking collectives: none -> 124 us  [exchange(): return lax.all_to_all(value, axes, 0, 0, tiled=True)]
    scatter-add x12 -> x0, other arithmetic: 53.4 us -> none  [add_group(): return running.at[places].add(contrib)]
    gather x12 -> x0, local copies, waits for them, and re-layouts: 24.3 us -> none  [add_group(): tile_rows = jnp.take(source, pick_rows, axis=0)]
    dot_general x14 -> x0, matrix products: 21 us -> none  [the longest x12 18.5 us: add_group(): jnp.einsum(pattern, chosen, tile_rows, preferred_element_type=jnp.float32)]
    all_to_all x0 -> x1, waiting for transfers between devices: none -> 20.9 us  [exchange(): return lax.all_to_all(value, axes, 0, 0, tiled=True)]
    ppermute x0 -> x2, starting transfers between devices: none -> 15.1 us  [other_core(): return lax.ppermute(value, 'core', [(0, 1), (1, 0)])]
  transfers between devices with their start and end apart: 4 -> 3, of which waited for: 4 -> 3; matrix products, arithmetic and copies ran while one was open for 0% -> 1% of each run, Pallas kernels for 0% -> 0%
where the time goes in v1:
time: 201 us
  blocking collectives  124 us (62%)
  starting transfers between devices  29.6 us (15%)
  waiting for transfers between devices  22.6 us (11%)
  Pallas kernels  14.6 us (7%)
  other arithmetic  4.47 us (2%)
  local copies, waits for them, and re-layouts  3.75 us (2%)
    all_to_all x5, blocking collectives, exchange(): return lax.all_to_all(value, axes, 0, 0, tiled=True)  124 us
    all_to_all x1, waiting for transfers between devices, exchange(): return lax.all_to_all(value, axes, 0, 0, tiled=True)  20.9 us
    ppermute x2, starting transfers between devices, other_core(): return lax.ppermute(value, 'core', [(0, 1), (1, 0)])  15.1 us
    all_to_all x1, starting transfers between devices, exchange(): return lax.all_to_all(value, axes, 0, 0, tiled=True)  14.5 us
    pallas_call x2, Pallas kernels, spmm(): pl.pallas_call(body, out_shape=jax.ShapeDtypeStruct((blocks, BSZ, HID), j...  12.3 us
  transfers between devices with their start and end apart: 3, of which 3 were waited for; matrix products, arithmetic and copies ran while one was open for 1% of the time, Pallas kernels for 0%

profile of v1, /device:TPU:1, one launch (start us, length us, event | category | flops | bytes accessed | tf_op | source)
XLA Modules:
  0.0 200.5 jit_solution(8388288350267479858)
XLA Ops:
  0.6 0.7 convert_multiply_fusion
  1.3 0.9 multiply_convert_fusion.1
  2.3 16.7 %all_to_all.30.rest_0_ = bf16[8,128,256]{2,1,0:T(8,128)(2,1)S(1)} all-to-all(bf16[8,128,256]{2,1,0:T(8,128)(2,1)S(1)} %broadcast_in_dim.6), channel_id=1, replica_groups=mesh['y'=4,'xh'=2,'core'=2,'zh'=8,'zl'=2,'xl'=2] {'y','xh'}, dimensions={0} | all-to-all | bytes 1048576 | tf_op jit(solution)/shard_map/all_to_all | solution.py:135
  18.9 5.0 %collective-permute-start = (bf16[8,128,256]{2,1,0:T(8,128)(2,1)S(1)}, bf16[8,128,256]{2,1,0:T(8,128)(2,1)S(1)}, u32[]{:S(2)}, u32[]{:S(2)}) collective-permute-start(bf16[8,128,256]{2,1,0:T(8,128)(2,1)S(1)} %all_to_all.30.rest_0_), channel_id=1, source_target_pairs={{0,32},{32,0},{1,33},{33,1},{2,34},{34,2},{3,35},{35,3},{4,36},{36... | collective-permute-start | bytes 1572872 | tf_op jit(solution)/shard_map/ppermute | solution.py:139
  24.7 0.7 add_bitcast_fusion
  25.3 0.2 collective-permute-done.rest_1_
  25.5 0.0 copy-start
  25.5 1.9 copy-done
  27.4 6.7 %shard_map.104 = bf16[32,128,256]{2,1,0:T(8,128)(2,1)S(1)} custom-call(s32[1]{0:T(128)} %bitcast.10.count_ref, s32[96]{0:T(128)S(1)} %get-tuple-element.10.src_ref.dst_ref, s32[96]{0:T(128)S(1)} %get-tuple-element.9.dst_ref.src_ref, bf16[96,128,128]{2,1,0:T(8,128)(2,1)S(1)} %bitcast.12, bf16[8,128,256]{2,1,0:T(8,128)(2,1)S(1)} %all_to_all.30.rest_0_, ...), custom_call_target="tpu_custom_call" | custom-call | flops 805306368 | bytes 3145728 | tf_op jit(solution)/shard_map/pallas_call | solution.py:87
  34.1 26.0 %all_to_all.31 = bf16[32,128,256]{2,1,0:T(8,128)(2,1)S(1)} all-to-all(bf16[32,128,256]{2,1,0:T(8,128)(2,1)S(1)} %shard_map.104), channel_id=1, replica_groups=mesh['y'=4,'xh'=2,'core'=2,'zh'=8,'zl'=2,'xl'=2] {'zl','xl'}, dimensions={0} | all-to-all | bytes 4194304 | tf_op jit(solution)/shard_map/all_to_all | solution.py:135
  60.1 1.3 reduce_sum.21
  61.4 14.5 %all-to-all-start.2 = ((bf16[8,128,256]{2,1,0:T(8,128)(2,1)}), bf16[8,128,256]{2,1,0:T(8,128)(2,1)S(1)}, u32[]{:S(2)}, u32[]{:S(2)}) async-start(bf16[8,128,256]{2,1,0:T(8,128)(2,1)} %reduce_sum.21), calls=%async_computation.2 | async-start | bytes 1048576 | tf_op jit(solution)/shard_map/all_to_all | solution.py:135
  75.9 0.7 copy.11.norm_ref
  76.6 20.9 %all-to-all-done.2.parts_ref = bf16[8,128,256]{2,1,0:T(8,128)(2,1)S(1)} async-done(((bf16[8,128,256]{2,1,0:T(8,128)(2,1)}), bf16[8,128,256]{2,1,0:T(8,128)(2,1)S(1)}, u32[]{:S(2)}, u32[]{:S(2)}) %all-to-all-start.2) | async-done | bytes 524320 | tf_op jit(solution)/shard_map/all_to_all | solution.py:135
  97.5 0.0 copy-start.2
  97.5 0.8 copy-done.2
  98.3 2.3 %shard_map.105 = (bf16[128,256]{1,0:T(8,128)(2,1)}, bf16[8,128,256]{2,1,0:T(8,128)(2,1)}) custom-call(bf16[8,128,256]{2,1,0:T(8,128)(2,1)} %copy-done.2, f32[128,1]{1,0:T(8,128)} %copy.11.norm_ref, bf16[256,256]{1,0:T(8,128)(2,1)} %weight_ref.1, bf16[128,256]{1,0:T(8,128)(2,1)} %cotangent_ref.1), custom_call_target="tpu_custom_call" | custom-call | tf_op jit(solution)/shard_map/pallas_call | solution.py:123
  100.6 26.4 %all_to_all.32 = bf16[8,128,256]{2,1,0:T(8,128)(2,1)S(1)} all-to-all(bf16[8,128,256]{2,1,0:T(8,128)(2,1)} %get-tuple-element.5), channel_id=1, replica_groups=mesh['y'=4,'xh'=2,'core'=2,'zh'=8,'zl'=2,'xl'=2] {'zh'}, dimensions={0} | all-to-all | bytes 1048576 | tf_op jit(solution)/shard_map/all_to_all | solution.py:135
  127.0 0.2 broadcast_in_dim.8
  127.3 0.0 copy-start.1
  127.3 36.7 %all_to_all.33.rest_0_ = bf16[32,128,256]{2,1,0:T(8,128)(2,1)S(1)} all-to-all(bf16[32,128,256]{2,1,0:T(8,128)(2,1)S(1)} %bitcast.14), channel_id=1, replica_groups=mesh['y'=4,'xh'=2,'core'=2,'zh'=8,'zl'=2,'xl'=2] {'zl','xl'}, dimensions={0} | all-to-all | bytes 4194304 | tf_op jit(solution)/shard_map/all_to_all | solution.py:135
  164.0 0.0 copy-done.1
  164.0 5.7 %shard_map.106 = bf16[16,128,256]{2,1,0:T(8,128)(2,1)S(1)} custom-call(s32[1]{0:T(128)} %bitcast.11.count_ref, s32[96]{0:T(128)S(1)} %get-tuple-element.9.dst_ref.src_ref, s32[96]{0:T(128)S(1)} %get-tuple-element.10.src_ref.dst_ref, bf16[96,128,128]{2,1,0:T(8,128)(2,1)S(1)} %bitcast.13, bf16[32,128,256]{2,1,0:T(8,128)(2,1)S(1)} %all_to_all.33.rest_0_), custom_call_target="tpu_custom_call" | custom-call | flops 805306368 | bytes 3145728 | tf_op jit(solution)/shard_map/pallas_call | solution.py:87
  169.7 10.0 %collective-permute-start.1 = (bf16[8,128,256]{2,1,0:T(8,128)(2,1)S(1)}, bf16[8,128,256]{2,1,0:T(8,128)(2,1)S(1)}, u32[]{:S(2)}, u32[]{:S(2)}) collective-permute-start(bf16[8,128,256]{2,1,0:T(8,128)(2,1)S(1)} %slice.9), channel_id=1, source_target_pairs={{0,32},{32,0},{1,33},{33,1},{2,34},{34,2},{3,35},{35,3},{4,36},{36... | collective-permute-start | bytes 1572872 | tf_op jit(solution)/shard_map/ppermute | solution.py:139
  179.8 1.5 collective-permute-done.1
  181.3 0.1 add_convert_fusion
  181.4 18.3 %all_to_all.34 = bf16[8,128,256]{2,1,0:T(8,128)(2,1)S(1)} all-to-all(bf16[8,128,256]{2,1,0:T(8,128)(2,1)S(1)} %add_convert_fusion), channel_id=1, replica_groups=mesh['y'=4,'xh'=2,'core'=2,'zh'=8,'zl'=2,'xl'=2] {'y','xh'}, dimensions={0} | all-to-all | bytes 1048576 | tf_op jit(solution)/shard_map/all_to_all | solution.py:135
  199.7 0.1 convert_reduce_fusion
  199.8 0.7 multiply_convert_fusion
  (2 shorter events, 0.1 us)
Async XLA Ops:
  18.9 6.6 %collective-permute-start = (bf16[8,128,256]{2,1,0:T(8,128)(2,1)S(1)}, bf16[8,128,256]{2,1,0:T(8,128)(2,1)S(1)}, u32[]{:S(2)}, u32[]{:S(2)}) collective-permute-start(bf16[8,128,256]{2,1,0:T(8,128)(2,1)S(1)} %all_to_all.30.rest_0_), channel_id=1, source_target_pairs={{0,32},{32,0},{1,33},{33,1},{2,34},{34,2},{3,35},{35,3},{4,36},{36... | collective-permute-start | bytes 1572872 | tf_op jit(solution)/shard_map/ppermute | solution.py:139
  25.5 1.9 copy-start
  61.4 36.2 %all-to-all-start.2 = ((bf16[8,128,256]{2,1,0:T(8,128)(2,1)}), bf16[8,128,256]{2,1,0:T(8,128)(2,1)S(1)}, u32[]{:S(2)}, u32[]{:S(2)}) async-start(bf16[8,128,256]{2,1,0:T(8,128)(2,1)} %reduce_sum.21), calls=%async_computation.2 | async-start | bytes 1048576 | tf_op jit(solution)/shard_map/all_to_all | solution.py:135
  97.5 0.8 copy-start.2
  127.3 36.7 %copy-start.1 = (bf16[1,1,96,128,128]{4,3,2,1,0:T(8,128)(2,1)S(1)}, bf16[1,1,96,128,128]{4,3,2,1,0:T(8,128)(2,1)}, u32[]{:S(2)}) copy-start(bf16[1,1,96,128,128]{4,3,2,1,0:T(8,128)(2,1)} %param.17) | copy-start | bytes 9437188
  169.7 11.5 %collective-permute-start.1 = (bf16[8,128,256]{2,1,0:T(8,128)(2,1)S(1)}, bf16[8,128,256]{2,1,0:T(8,128)(2,1)S(1)}, u32[]{:S(2)}, u32[]{:S(2)}) collective-permute-start(bf16[8,128,256]{2,1,0:T(8,128)(2,1)S(1)} %slice.9), channel_id=1, source_target_pairs={{0,32},{32,0},{1,33},{33,1},{2,34},{34,2},{3,35},{35,3},{4,36},{36... | collective-permute-start | bytes 1572872 | tf_op jit(solution)/shard_map/ppermute | solution.py:139

commit v2 on v1

--- a/solution.py
+++ b/solution.py
@@ -71,6 +71,7 @@
 
 def spmm(transposed, count, src, dst, edges, first, second, blocks):
     slots = edges.shape[0]
+    wide = first.shape[2]
     vmem = pl.BlockSpec(memory_space=pltpu.VMEM)
     smem = pl.BlockSpec(memory_space=pltpu.SMEM)
     tables = [first] if second is None else [first, second]
@@ -86,18 +87,18 @@
     table_rows = 1 if second is None else 2 * first.shape[0]
     return pl.pallas_call(
         body,
-        out_shape=jax.ShapeDtypeStruct((blocks, BSZ, HID), jnp.bfloat16),
-        in_specs=[smem, smem, smem, pl.BlockSpec(memory_space=pl.ANY)] + [vmem] * len(tables),
+        out_shape=jax.ShapeDtypeStruct((blocks, BSZ, wide), jnp.bfloat16),
+        in_specs=[smem, smem, smem, pl.BlockSpec(memory_space=pltpu.HBM)] + [vmem] * len(tables),
         out_specs=vmem,
         scratch_shapes=[
             pltpu.VMEM((slots, BSZ, BSZ), jnp.bfloat16),
-            pltpu.VMEM((table_rows, BSZ, HID), jnp.bfloat16),
-            pltpu.VMEM((blocks + 1, BSZ, HID), jnp.float32),
+            pltpu.VMEM((table_rows, BSZ, wide), jnp.bfloat16),
+            pltpu.VMEM((blocks + 1, BSZ, wide), jnp.float32),
             pltpu.SemaphoreType.DMA((slots // CHUNK,)),
         ],
-        compiler_params=pltpu.CompilerParams(vmem_limit_bytes=32 * 1024 * 1024),
+        compiler_params=pltpu.CompilerParams(vmem_limit_bytes=57 * 1024 * 1024),
         cost_estimate=pl.CostEstimate(
-            flops=2 * slots * BSZ * BSZ * HID, bytes_accessed=2 * slots * BSZ * BSZ, transcendentals=0
+            flops=16 * slots * BSZ * BSZ * HID, bytes_accessed=2 * slots * BSZ * BSZ, transcendentals=0
         ),
     )(count, src, dst, edges, *tables)
 
@@ -113,21 +114,20 @@
     slope = gate * (1.0 + preact * (1.0 - gate))
     dpre = (cotangent_ref[...].astype(jnp.float32) * slope).astype(jnp.bfloat16)
     back = lax.dot_general(dpre, weight, (((1,), (1,)), ((), ())), preferred_element_type=jnp.float32)
-    back = (back * norm).astype(jnp.bfloat16)
-    for i in range(back_ref.shape[0]):
-        back_ref[i] = back
-
-
-def middle(parts, norm, weight, cotangent, copies):
+    back_ref[...] = (back * norm).astype(jnp.bfloat16)
+
+
+def middle(parts, norm, weight, cotangent):
     vmem = pl.BlockSpec(memory_space=pltpu.VMEM)
     return pl.pallas_call(
         middle_kernel,
         out_shape=(
             jax.ShapeDtypeStruct(cotangent.shape, jnp.bfloat16),
-            jax.ShapeDtypeStruct((copies,) + cotangent.shape, jnp.bfloat16),
+            jax.ShapeDtypeStruct(cotangent.shape, jnp.bfloat16),
         ),
         in_specs=[vmem] * 4,
         out_specs=(vmem, vmem),
+        compiler_params=pltpu.CompilerParams(vmem_limit_bytes=12 * 1024 * 1024),
     )(parts, norm, weight, cotangent)
 
 
@@ -137,6 +137,10 @@
 
 def other_core(value):
     return lax.ppermute(value, "core", [(0, 1), (1, 0)])
+
+
+def copies(value, number):
+    return jnp.broadcast_to(value[None], (number,) + value.shape)
 
 
 def add_up(value):
@@ -157,21 +161,26 @@
     row_at = (rows & 3) * 8 + (rows >> 2)
     col_at = ((cols & 1) ^ core) * 8 + (cols >> 1)
 
-    mine = exchange(jnp.broadcast_to(scaled[None], (8, BSZ, HID)), ("y", "xh"))
-    theirs = other_core(mine)
-    partial = spmm(True, count, col_at, row_at, edges, mine, theirs, 32)
-    near = exchange(partial, ("zl", "xl"))
-    near = add_up(near.reshape(4, 8, BSZ, HID)).astype(jnp.bfloat16)
-    far = exchange(near, ("zh",))
-    activated, back = middle(far, norm, weight, cotangent, 8)
-
-    back = exchange(back, ("zh",))
-    back = exchange(jnp.broadcast_to(back[None], (4, 8, BSZ, HID)).reshape(32, BSZ, HID), ("zl", "xl"))
-    partial = spmm(False, count, row_at, col_at, edges, back, None, 16)
-    received = other_core(partial[8:])
-    pair = (partial[:8].astype(jnp.float32) + received.astype(jnp.float32)).astype(jnp.bfloat16)
-    pair = exchange(pair, ("y", "xh"))
-    grad_hidden = (add_up(pair) * norm).astype(jnp.bfloat16)
+    halves = (slice(0, HID // 2), slice(HID // 2, HID))
+    mine = [exchange(copies(scaled[:, h], 8), ("y", "xh")) for h in halves]
+    near = []
+    for part in mine:
+        partial = spmm(True, count, col_at, row_at, edges, part, other_core(part), 32)
+        received = exchange(partial, ("zl", "xl"))
+        near.append(add_up(received.reshape(4, 8, BSZ, HID // 2)).astype(jnp.bfloat16))
+    far = exchange(jnp.concatenate(near, axis=2), ("zh",))
+    activated, back = middle(far, norm, weight, cotangent)
+
+    back = lax.all_gather(back, "zh", axis=0)
+    grads = []
+    for h in halves:
+        table = exchange(copies(back[:, :, h], 4).reshape(32, BSZ, HID // 2), ("zl", "xl"))
+        partial = spmm(False, count, row_at, col_at, edges, table, None, 16)
+        received = other_core(partial[8:])
+        pair = (partial[:8].astype(jnp.float32) + received.astype(jnp.float32)).astype(jnp.bfloat16)
+        pair = exchange(pair, ("y", "xh"))
+        grads.append((add_up(pair) * norm).astype(jnp.bfloat16))
+    grad_hidden = jnp.concatenate(grads, axis=1)
     return activated, grad_hidden
 
 

time: 201 us -> 219 us (1.090)
  the two profiles are of different devices: /device:TPU:1 before, /device:TPU:2 now
where the time goes in v2:
time: 219 us; the launch traced here: 217 us
  blocking collectives  63.4 us (29%)
  waiting for transfers between devices  57.7 us (26%)
  starting transfers between devices  53.7 us (25%)
  Pallas kernels  26.9 us (12%)
  other arithmetic  7.37 us (3%)
  local copies, waits for them, and re-layouts  6.83 us (3%)
    all_to_all x7, waiting for transfers between devices, exchange(): return lax.all_to_all(value, axes, 0, 0, tiled=True)  56.2 us
    all_to_all x7, starting transfers between devices, exchange(): return lax.all_to_all(value, axes, 0, 0, tiled=True)  46 us
    all_gather x1, blocking collectives, per_device(): back = lax.all_gather(back, 'zh', axis=0)  34.8 us
    all_to_all x2, blocking collectives, exchange(): return lax.all_to_all(value, axes, 0, 0, tiled=True)  28.6 us
    pallas_call x4, Pallas kernels, spmm(): pl.pallas_call(body, out_shape=jax.ShapeDtypeStruct((blocks, BSZ, wide),...  26 us
    ppermute x4, starting transfers between devices, other_core(): return lax.ppermute(value, 'core', [(0, 1), (1, 0)])  7.66 us
  transfers between devices with their start and end apart: 11, of which 7 were waited for; matrix products, arithmetic and copies ran while one was open for 3% of the time, Pallas kernels for 12%

profile of v2, /device:TPU:2, one launch (start us, length us, event | category | flops | bytes accessed | tf_op | source)
XLA Modules:
  0.0 217.3 jit_solution(14350699922514647510)
XLA Ops:
  1.3 0.9 multiply_convert_fusion
  2.3 14.6 %all_to_all.45.rest_0_ = bf16[8,128,128]{2,1,0:T(8,128)(2,1)S(1)} all-to-all(bf16[8,128,128]{2,1,0:T(8,128)(2,1)S(1)} %broadcast_in_dim.11), channel_id=1, replica_groups=mesh['y'=4,'xh'=2,'core'=2,'zh'=8,'zl'=2,'xl'=2] {'y','xh'}, dimensions={0} | all-to-all | bytes 524288 | tf_op jit(solution)/shard_map/all_to_all | solution.py:135
  16.9 1.9 collective-permute-start.1
  19.6 3.4 %all-to-all-start = ((bf16[8,128,128]{2,1,0:T(8,128)(2,1)}), bf16[8,128,128]{2,1,0:T(8,128)(2,1)S(1)}, u32[]{:S(2)}, u32[]{:S(2)}) async-start(bf16[8,128,128]{2,1,0:T(8,128)(2,1)} %broadcast_in_dim.10), calls=%async_computation | async-start | bytes 524288 | tf_op jit(solution)/shard_map/all_to_all | solution.py:135
  23.7 1.2 add_bitcast_fusion
  25.6 6.8 %shard_map.105 = bf16[32,128,128]{2,1,0:T(8,128)(2,1)} custom-call(s32[1]{0:T(128)} %bitcast.14.count_ref, s32[96]{0:T(128)} %get-tuple-element.16.src_ref.dst_ref, s32[96]{0:T(128)} %get-tuple-element.15.dst_ref.src_ref, bf16[96,128,128]{2,1,0:T(8,128)(2,1)} %bitcast.21, bf16[8,128,128]{2,1,0:T(8,128)(2,1)} %copy-done.5, bf16[8,128,128]{2,1,0:T(8,128)(2,1)} %copy-done.6), custom_call_target="tpu_custom_call" | custom-call | flops 6442450944 | bytes 3145728 | tf_op jit(solution)/shard_map/pallas_call | solution.py:88
  32.7 6.1 %all-to-all-start.3 = ((bf16[32,128,128]{2,1,0:T(8,128)(2,1)}), bf16[32,128,128]{2,1,0:T(8,128)(2,1)S(1)}, u32[]{:S(2)}, u32[]{:S(2)}) async-start(bf16[32,128,128]{2,1,0:T(8,128)(2,1)} %shard_map.105), calls=%async_computation.3 | async-start | bytes 2097152 | tf_op jit(solution)/shard_map/all_to_all | solution.py:135
  38.8 1.9 collective-permute-start
  40.7 1.5 collective-permute-done.rest_1_
  42.9 6.8 %shard_map.104 = bf16[32,128,128]{2,1,0:T(8,128)(2,1)} custom-call(s32[1]{0:T(128)} %bitcast.13.count_ref, s32[96]{0:T(128)} %get-tuple-element.16.src_ref.dst_ref, s32[96]{0:T(128)} %get-tuple-element.15.dst_ref.src_ref, bf16[96,128,128]{2,1,0:T(8,128)(2,1)} %bitcast.22, bf16[8,128,128]{2,1,0:T(8,128)(2,1)} %copy-done.4, bf16[8,128,128]{2,1,0:T(8,128)(2,1)} %copy-done.7), custom_call_target="tpu_custom_call" | custom-call | flops 6442450944 | bytes 3145728 | tf_op jit(solution)/shard_map/pallas_call | solution.py:88
  49.7 2.8 %all-to-all-done.3 = bf16[32,128,128]{2,1,0:T(8,128)(2,1)S(1)} async-done(((bf16[32,128,128]{2,1,0:T(8,128)(2,1)}), bf16[32,128,128]{2,1,0:T(8,128)(2,1)S(1)}, u32[]{:S(2)}, u32[]{:S(2)}) %all-to-all-start.3) | async-done | bytes 1048608 | tf_op jit(solution)/shard_map/all_to_all | solution.py:135
  52.6 4.0 %all-to-all-start.1 = ((bf16[32,128,128]{2,1,0:T(8,128)(2,1)}), bf16[32,128,128]{2,1,0:T(8,128)(2,1)S(1)}, u32[]{:S(2)}, u32[]{:S(2)}) async-start(bf16[32,128,128]{2,1,0:T(8,128)(2,1)} %shard_map.104), calls=%async_computation.1 | async-start | bytes 2097152 | tf_op jit(solution)/shard_map/all_to_all | solution.py:135
  56.8 12.7 %all-to-all-done.1 = bf16[32,128,128]{2,1,0:T(8,128)(2,1)S(1)} async-done(((bf16[32,128,128]{2,1,0:T(8,128)(2,1)}), bf16[32,128,128]{2,1,0:T(8,128)(2,1)S(1)}, u32[]{:S(2)}, u32[]{:S(2)}) %all-to-all-start.1) | async-done | bytes 1048608 | tf_op jit(solution)/shard_map/all_to_all | solution.py:135
  70.6 14.2 %all-to-all-start.4 = ((bf16[8,128,256]{2,1,0:T(8,128)(2,1)}), bf16[8,128,256]{2,1,0:T(8,128)(2,1)S(1)}, u32[]{:S(2)}, u32[]{:S(2)}) async-start(bf16[8,128,256]{2,1,0:T(8,128)(2,1)} %pad_maximum_fusion), calls=%async_computation.4 | async-start | bytes 1048576 | tf_op jit(solution)/shard_map/all_to_all | solution.py:135
  84.9 24.0 %all-to-all-done.4.parts_ref = bf16[8,128,256]{2,1,0:T(8,128)(2,1)S(1)} async-done(((bf16[8,128,256]{2,1,0:T(8,128)(2,1)}), bf16[8,128,256]{2,1,0:T(8,128)(2,1)S(1)}, u32[]{:S(2)}, u32[]{:S(2)}) %all-to-all-start.4) | async-done | bytes 524320 | tf_op jit(solution)/shard_map/all_to_all | solution.py:135
  108.9 0.9 shard_map.106
  109.8 34.8 %all-gather = bf16[1024,256]{1,0:T(8,128)(2,1)S(1)} all-gather(bf16[128,256]{1,0:T(8,128)(2,1)S(1)} %get-tuple-element.5), channel_id=2, replica_groups=mesh['y'=4,'xh'=2,'core'=2,'zh'=8,'zl'=2,'xl'=2] {'zh'}, dimensions={0}, use_global_device_ids=true | all-gather | bytes 589824 | tf_op jit(solution)/shard_map/all_gather | solution.py:174
  144.9 14.0 %all_to_all.46.rest_0_ = bf16[32,128,128]{2,1,0:T(8,128)(2,1)} all-to-all(bf16[32,128,128]{2,1,0:T(8,128)(2,1)S(1)} %bitcast.17), channel_id=1, replica_groups=mesh['y'=4,'xh'=2,'core'=2,'zh'=8,'zl'=2,'xl'=2] {'zl','xl'}, dimensions={0} | all-to-all | bytes 2097152 | tf_op jit(solution)/shard_map/all_to_all | solution.py:135
  158.9 1.2 broadcast_in_dim.14
  160.1 4.6 %all-to-all-start.7 = ((bf16[32,128,128]{2,1,0:T(8,128)(2,1)}), bf16[32,128,128]{2,1,0:T(8,128)(2,1)S(1)}, u32[]{:S(2)}, u32[]{:S(2)}) async-start(bf16[32,128,128]{2,1,0:T(8,128)(2,1)} %bitcast.9), calls=%async_computation.7 | async-start | bytes 2097152 | tf_op jit(solution)/shard_map/all_to_all | solution.py:135
  164.7 6.2 %shard_map.107 = bf16[16,128,128]{2,1,0:T(8,128)(2,1)} custom-call(s32[1]{0:T(128)} %bitcast.15.count_ref, s32[96]{0:T(128)} %get-tuple-element.15.dst_ref.src_ref, s32[96]{0:T(128)} %get-tuple-element.16.src_ref.dst_ref, bf16[96,128,128]{2,1,0:T(8,128)(2,1)} %bitcast.23, bf16[32,128,128]{2,1,0:T(8,128)(2,1)} %all_to_all.46.rest_0_), custom_call_target="tpu_custom_call" | custom-call | flops 6442450944 | bytes 3145728 | tf_op jit(solution)/shard_map/pallas_call | solution.py:88
  170.9 1.0 slice.36
  171.9 1.9 collective-permute-start.2
  173.8 1.0 copy-done.2
  174.8 6.2 %shard_map.108 = bf16[16,128,128]{2,1,0:T(8,128)(2,1)} custom-call(s32[1]{0:T(128)} %bitcast.16.count_ref, s32[96]{0:T(128)} %get-tuple-element.15.dst_ref.src_ref, s32[96]{0:T(128)} %get-tuple-element.16.src_ref.dst_ref, bf16[96,128,128]{2,1,0:T(8,128)(2,1)} %bitcast.24, bf16[32,128,128]{2,1,0:T(8,128)(2,1)} %copy-done.2), custom_call_target="tpu_custom_call" | custom-call | flops 6442450944 | bytes 3145728 | tf_op jit(solution)/shard_map/pallas_call | solution.py:88
  181.0 1.0 slice.39
  182.0 1.9 collective-permute-start.3
  184.7 10.2 %all-to-all-start.6 = ((bf16[8,128,128]{2,1,0:T(8,128)(2,1)}), bf16[8,128,128]{2,1,0:T(8,128)(2,1)S(1)}, u32[]{:S(2)}, u32[]{:S(2)}) async-start(bf16[8,128,128]{2,1,0:T(8,128)(2,1)} %add_convert_fusion.1), calls=%async_computation.6 | async-start | bytes 524288 | tf_op jit(solution)/shard_map/all_to_all | solution.py:135
  194.9 1.7 add_convert_fusion
  196.6 7.7 %all-to-all-done.6 = bf16[8,128,128]{2,1,0:T(8,128)(2,1)S(1)} async-done(((bf16[8,128,128]{2,1,0:T(8,128)(2,1)}), bf16[8,128,128]{2,1,0:T(8,128)(2,1)S(1)}, u32[]{:S(2)}, u32[]{:S(2)}) %all-to-all-start.6) | async-done | bytes 262176 | tf_op jit(solution)/shard_map/all_to_all | solution.py:135
  204.4 3.4 %all-to-all-start.8 = ((bf16[8,128,128]{2,1,0:T(8,128)(2,1)}), bf16[8,128,128]{2,1,0:T(8,128)(2,1)S(1)}, u32[]{:S(2)}, u32[]{:S(2)}) async-start(bf16[8,128,128]{2,1,0:T(8,128)(2,1)} %add_convert_fusion), calls=%async_computation.8 | async-start | bytes 524288 | tf_op jit(solution)/shard_map/all_to_all | solution.py:135
  207.8 8.7 %all-to-all-done.8 = bf16[8,128,128]{2,1,0:T(8,128)(2,1)S(1)} async-done(((bf16[8,128,128]{2,1,0:T(8,128)(2,1)}), bf16[8,128,128]{2,1,0:T(8,128)(2,1)S(1)}, u32[]{:S(2)}, u32[]{:S(2)}) %all-to-all-start.8) | async-done | bytes 262176 | tf_op jit(solution)/shard_map/all_to_all | solution.py:135
  (35 shorter events, 6.5 us)
Async XLA Ops:
  16.9 8.0 %copy-start.5 = (bf16[8,128,128]{2,1,0:T(8,128)(2,1)}, bf16[8,128,128]{2,1,0:T(8,128)(2,1)S(1)}, u32[]{:S(2)}) copy-start(bf16[8,128,128]{2,1,0:T(8,128)(2,1)S(1)} %all_to_all.45.rest_0_) | copy-start | bytes 786436
  16.9 8.0 %collective-permute-start.1 = (bf16[8,128,128]{2,1,0:T(8,128)(2,1)S(1)}, bf16[8,128,128]{2,1,0:T(8,128)(2,1)S(1)}, u32[]{:S(2)}, u32[]{:S(2)}) collective-permute-start(bf16[8,128,128]{2,1,0:T(8,128)(2,1)S(1)} %all_to_all.45.rest_0_), channel_id=1, source_target_pairs={{0,32},{32,0},{1,33},{33,1},{2,34},{34,2},{3,35},{35,3},{4,36},{36... | collective-permute-start | bytes 786440 | tf_op jit(solution)/shard_map/ppermute | solution.py:139
  19.6 13.1 %all-to-all-start = ((bf16[8,128,128]{2,1,0:T(8,128)(2,1)}), bf16[8,128,128]{2,1,0:T(8,128)(2,1)S(1)}, u32[]{:S(2)}, u32[]{:S(2)}) async-start(bf16[8,128,128]{2,1,0:T(8,128)(2,1)} %broadcast_in_dim.10), calls=%async_computation | async-start | bytes 524288 | tf_op jit(solution)/shard_map/all_to_all | solution.py:135
  24.9 0.7 copy-start.6
  32.7 9.6 %copy-start.4 = (bf16[8,128,128]{2,1,0:T(8,128)(2,1)}, bf16[8,128,128]{2,1,0:T(8,128)(2,1)S(1)}, u32[]{:S(2)}) copy-start(bf16[8,128,128]{2,1,0:T(8,128)(2,1)S(1)} %all-to-all-done.rest_0_) | copy-start | bytes 786436
  32.7 19.9 %all-to-all-start.3 = ((bf16[32,128,128]{2,1,0:T(8,128)(2,1)}), bf16[32,128,128]{2,1,0:T(8,128)(2,1)S(1)}, u32[]{:S(2)}, u32[]{:S(2)}) async-start(bf16[32,128,128]{2,1,0:T(8,128)(2,1)} %shard_map.105), calls=%async_computation.3 | async-start | bytes 2097152 | tf_op jit(solution)/shard_map/all_to_all | solution.py:135
  38.8 3.4 %collective-permute-start = (bf16[8,128,128]{2,1,0:T(8,128)(2,1)S(1)}, bf16[8,128,128]{2,1,0:T(8,128)(2,1)S(1)}, u32[]{:S(2)}, u32[]{:S(2)}) collective-permute-start(bf16[8,128,128]{2,1,0:T(8,128)(2,1)S(1)} %all-to-all-done.rest_0_), channel_id=1, source_target_pairs={{0,32},{32,0},{1,33},{33,1},{2,34},{34,2},{3,35},{35,3},{4,36},{36... | collective-permute-start | bytes 786440 | tf_op jit(solution)/shard_map/ppermute | solution.py:139
  42.2 0.7 copy-start.7
  49.7 59.2 %copy-start = (bf16[256,256]{1,0:T(8,128)(2,1)S(1)}, bf16[256,256]{1,0:T(8,128)(2,1)}, u32[]{:S(2)}) copy-start(bf16[256,256]{1,0:T(8,128)(2,1)} %weight_ref.1) | copy-start | bytes 393220
  49.7 59.2 %copy-start.1 = (bf16[128,256]{1,0:T(8,128)(2,1)S(1)}, bf16[128,256]{1,0:T(8,128)(2,1)}, u32[]{:S(2)}) copy-start(bf16[128,256]{1,0:T(8,128)(2,1)} %cotangent_ref.1) | copy-start | bytes 196612
  52.6 17.0 %all-to-all-start.1 = ((bf16[32,128,128]{2,1,0:T(8,128)(2,1)}), bf16[32,128,128]{2,1,0:T(8,128)(2,1)S(1)}, u32[]{:S(2)}, u32[]{:S(2)}) async-start(bf16[32,128,128]{2,1,0:T(8,128)(2,1)} %shard_map.104), calls=%async_computation.1 | async-start | bytes 2097152 | tf_op jit(solution)/shard_map/all_to_all | solution.py:135
  70.6 38.3 %all-to-all-start.4 = ((bf16[8,128,256]{2,1,0:T(8,128)(2,1)}), bf16[8,128,256]{2,1,0:T(8,128)(2,1)S(1)}, u32[]{:S(2)}, u32[]{:S(2)}) async-start(bf16[8,128,256]{2,1,0:T(8,128)(2,1)} %pad_maximum_fusion), calls=%async_computation.4 | async-start | bytes 1048576 | tf_op jit(solution)/shard_map/all_to_all | solution.py:135
  160.1 13.7 %all-to-all-start.7 = ((bf16[32,128,128]{2,1,0:T(8,128)(2,1)}), bf16[32,128,128]{2,1,0:T(8,128)(2,1)S(1)}, u32[]{:S(2)}, u32[]{:S(2)}) async-start(bf16[32,128,128]{2,1,0:T(8,128)(2,1)} %bitcast.9), calls=%async_computation.7 | async-start | bytes 2097152 | tf_op jit(solution)/shard_map/all_to_all | solution.py:135
  171.9 12.1 %collective-permute-start.2 = (bf16[8,128,128]{2,1,0:T(8,128)(2,1)S(1)}, bf16[8,128,128]{2,1,0:T(8,128)(2,1)S(1)}, u32[]{:S(2)}, u32[]{:S(2)}) collective-permute-start(bf16[8,128,128]{2,1,0:T(8,128)(2,1)S(1)} %slice.36), channel_id=1, source_target_pairs={{0,32},{32,0},{1,33},{33,1},{2,34},{34,2},{3,35},{35,3},{4,36},{36... | collective-permute-start | bytes 786440 | tf_op jit(solution)/shard_map/ppermute | solution.py:139
  173.8 1.0 copy-start.2
  174.8 9.2 %copy-start.3 = (bf16[16,128,128]{2,1,0:T(8,128)(2,1)S(1)}, bf16[16,128,128]{2,1,0:T(8,128)(2,1)}, u32[]{:S(2)}) copy-start(bf16[16,128,128]{2,1,0:T(8,128)(2,1)} %shard_map.107) | copy-start | bytes 1572868
  182.0 12.9 %collective-permute-start.3 = (bf16[8,128,128]{2,1,0:T(8,128)(2,1)S(1)}, bf16[8,128,128]{2,1,0:T(8,128)(2,1)S(1)}, u32[]{:S(2)}, u32[]{:S(2)}) collective-permute-start(bf16[8,128,128]{2,1,0:T(8,128)(2,1)S(1)} %slice.39), channel_id=1, source_target_pairs={{0,32},{32,0},{1,33},{33,1},{2,34},{34,2},{3,35},{35,3},{4,36},{36... | collective-permute-start | bytes 786440 | tf_op jit(solution)/shard_map/ppermute | solution.py:139
  184.7 19.6 %all-to-all-start.6 = ((bf16[8,128,128]{2,1,0:T(8,128)(2,1)}), bf16[8,128,128]{2,1,0:T(8,128)(2,1)S(1)}, u32[]{:S(2)}, u32[]{:S(2)}) async-start(bf16[8,128,128]{2,1,0:T(8,128)(2,1)} %add_convert_fusion.1), calls=%async_computation.6 | async-start | bytes 524288 | tf_op jit(solution)/shard_map/all_to_all | solution.py:135
  204.4 12.1 %all-to-all-start.8 = ((bf16[8,128,128]{2,1,0:T(8,128)(2,1)}), bf16[8,128,128]{2,1,0:T(8,128)(2,1)S(1)}, u32[]{:S(2)}, u32[]{:S(2)}) async-start(bf16[8,128,128]{2,1,0:T(8,128)(2,1)} %add_convert_fusion), calls=%async_computation.8 | async-start | bytes 524288 | tf_op jit(solution)/shard_map/all_to_all | solution.py:135

commit v3 on v1

--- a/solution.py
+++ b/solution.py
@@ -10,7 +10,8 @@
 HID = 256
 BSZ = 128
 QDEN = 192
-GROUP = 4
+GROUP = 16
+AHEAD = 1
 CHUNK = 16
 
 NAMES = ("y", "xh", "core", "zh", "zl", "xl")
@@ -51,17 +52,18 @@
             def step(g, carry):
                 base = c * CHUNK + g * GROUP
                 products = []
-                for u in range(GROUP):
-                    k = base + u
-                    products.append(
-                        lax.dot_general(
-                            edge_buf[k], source[src_ref[k]], contract, preferred_element_type=jnp.float32
+                for u in range(GROUP + AHEAD):
+                    if u < GROUP:
+                        k = base + u
+                        products.append(
+                            lax.dot_general(
+                                edge_buf[k], source[src_ref[k]], contract, preferred_element_type=jnp.float32
+                            )
                         )
-                    )
-                for u in range(GROUP):
-                    k = base + u
-                    place = jnp.where(k < count, dst_ref[k], blocks)
-                    acc[place] += products[u]
+                    if u >= AHEAD:
+                        k = base + u - AHEAD
+                        place = jnp.where(k < count, dst_ref[k], blocks)
+                        acc[place] += products[u - AHEAD]
                 return carry
 
             lax.fori_loop(0, CHUNK // GROUP, step, 0)
@@ -95,7 +97,7 @@
             pltpu.VMEM((blocks + 1, BSZ, HID), jnp.float32),
             pltpu.SemaphoreType.DMA((slots // CHUNK,)),
         ],
-        compiler_params=pltpu.CompilerParams(vmem_limit_bytes=32 * 1024 * 1024),
+        compiler_params=pltpu.CompilerParams(vmem_limit_bytes=48 * 1024 * 1024),
         cost_estimate=pl.CostEstimate(
             flops=2 * slots * BSZ * BSZ * HID, bytes_accessed=2 * slots * BSZ * BSZ, transcendentals=0
         ),
@@ -113,21 +115,24 @@
     slope = gate * (1.0 + preact * (1.0 - gate))
     dpre = (cotangent_ref[...].astype(jnp.float32) * slope).astype(jnp.bfloat16)
     back = lax.dot_general(dpre, weight, (((1,), (1,)), ((), ())), preferred_element_type=jnp.float32)
-    back = (back * norm).astype(jnp.bfloat16)
-    for i in range(back_ref.shape[0]):
-        back_ref[i] = back
-
-
-def middle(parts, norm, weight, cotangent, copies):
+    back = (back * norm).astype(jnp.bfloat16).astype(jnp.float32)
+    largest = jnp.maximum(jnp.max(jnp.abs(back), axis=(0, 1), keepdims=True), 1e-30)
+    power = 14.0 - jnp.floor(jnp.log2(largest))
+    back_ref[:BSZ] = back * jnp.exp2(power)
+    back_ref[BSZ:] = jnp.broadcast_to(power, (8, HID))
+
+
+def middle(parts, norm, weight, cotangent):
     vmem = pl.BlockSpec(memory_space=pltpu.VMEM)
     return pl.pallas_call(
         middle_kernel,
         out_shape=(
             jax.ShapeDtypeStruct(cotangent.shape, jnp.bfloat16),
-            jax.ShapeDtypeStruct((copies,) + cotangent.shape, jnp.bfloat16),
+            jax.ShapeDtypeStruct((BSZ + 8, HID), jnp.float32),
         ),
         in_specs=[vmem] * 4,
         out_specs=(vmem, vmem),
+        compiler_params=pltpu.CompilerParams(vmem_limit_bytes=12 * 1024 * 1024),
     )(parts, norm, weight, cotangent)
 
 
@@ -137,6 +142,14 @@
 
 def other_core(value):
     return lax.ppermute(value, "core", [(0, 1), (1, 0)])
+
+
+def gather_scaled(value):
+    sent = value.astype(jnp.float16)
+    pair = jnp.concatenate([sent, lax.ppermute(sent, "xl", [(0, 1), (1, 0)])], axis=0)
+    pairs = lax.all_gather(pair, ("zh", "zl"), axis=0, tiled=True).reshape(32, BSZ + 8, HID)
+    back = jnp.exp2(-pairs[:, BSZ : BSZ + 1, :1].astype(jnp.float32))
+    return (pairs[:, :BSZ].astype(jnp.float32) * back).astype(jnp.bfloat16)
 
 
 def add_up(value):
@@ -155,6 +168,7 @@
     cols = block_cols[0, 0]
     count = block_count[0]
     row_at = (rows & 3) * 8 + (rows >> 2)
+    row_to = (rows & ~1) + ((rows & 1) ^ lax.axis_index("xl"))
     col_at = ((cols & 1) ^ core) * 8 + (cols >> 1)
 
     mine = exchange(jnp.broadcast_to(scaled[None], (8, BSZ, HID)), ("y", "xh"))
@@ -163,11 +177,10 @@
     near = exchange(partial, ("zl", "xl"))
     near = add_up(near.reshape(4, 8, BSZ, HID)).astype(jnp.bfloat16)
     far = exchange(near, ("zh",))
-    activated, back = middle(far, norm, weight, cotangent, 8)
-
-    back = exchange(back, ("zh",))
-    back = exchange(jnp.broadcast_to(back[None], (4, 8, BSZ, HID)).reshape(32, BSZ, HID), ("zl", "xl"))
-    partial = spmm(False, count, row_at, col_at, edges, back, None, 16)
+    activated, back = middle(far, norm, weight, cotangent)
+
+    table = gather_scaled(back)
+    partial = spmm(False, count, row_to, col_at, edges, table, None, 16)
     received = other_core(partial[8:])
     pair = (partial[:8].astype(jnp.float32) + received.astype(jnp.float32)).astype(jnp.bfloat16)
     pair = exchange(pair, ("y", "xh"))

time: 201 us -> 178 us (0.89)
  blocking collectives: 124 us -> 95.4 us
  starting transfers between devices: 29.6 us -> 36.3 us
  waiting for transfers between devices: 22.6 us -> 28.6 us
  Pallas kernels: 14.6 us -> 9.9 us
  local copies, waits for them, and re-layouts: 3.75 us -> 0.19 us
    all_to_all x5 -> x3, blocking collectives: 124 us -> 57.6 us  [exchange(): return lax.all_to_all(value, axes, 0, 0, tiled=True)]
    all_gather x0 -> x1, blocking collectives: none -> 37.8 us  [gather_scaled(): lax.all_gather(pair, ('zh', 'zl'), axis=0, tiled=True)]
    ppermute x0 -> x1, starting transfers between devices: none -> 7.28 us  [gather_scaled(): lax.ppermute(sent, 'xl', [(0, 1), (1, 0)])]
    all_to_all x1, waiting for transfers between devices: 20.9 us -> 25.2 us  [exchange(): return lax.all_to_all(value, axes, 0, 0, tiled=True)]
    pallas_call x2, Pallas kernels: 12.3 us -> 9.04 us  [spmm(): pl.pallas_call(body, out_shape=jax.ShapeDtypeStruct((blocks, BSZ, HID), j...]
    unnamed x6 -> x4, local copies, waits for them, and re-layouts: 2.69 us -> 0.01 us
  transfers between devices with their start and end apart: 3 -> 4, of which waited for: 3 -> 4; matrix products, arithmetic and copies ran while one was open for 1% -> 0% of each run, Pallas kernels for 0% -> 0%
where the time goes in v3:
time: 178 us; the launch traced here: 177 us
  blocking collectives  95.4 us (54%)
  starting transfers between devices  36.3 us (20%)
  waiting for transfers between devices  28.6 us (16%)
  Pallas kernels  9.9 us (6%)
  other arithmetic  5.72 us (3%)
    all_to_all x3, blocking collectives, exchange(): return lax.all_to_all(value, axes, 0, 0, tiled=True)  57.6 us
    all_gather x1, blocking collectives, gather_scaled(): lax.all_gather(pair, ('zh', 'zl'), axis=0, tiled=True)  37.8 us
    all_to_all x1, waiting for transfers between devices, exchange(): return lax.all_to_all(value, axes, 0, 0, tiled=True)  25.2 us
    ppermute x2, starting transfers between devices, other_core(): return lax.ppermute(value, 'core', [(0, 1), (1, 0)])  14.6 us
    all_to_all x1, starting transfers between devices, exchange(): return lax.all_to_all(value, axes, 0, 0, tiled=True)  14.4 us
    pallas_call x2, Pallas kernels, spmm(): pl.pallas_call(body, out_shape=jax.ShapeDtypeStruct((blocks, BSZ, HID), j...  9.04 us
    ppermute x1, starting transfers between devices, gather_scaled(): lax.ppermute(sent, 'xl', [(0, 1), (1, 0)])  7.28 us
  transfers between devices with their start and end apart: 4, of which 4 were waited for; matrix products, arithmetic and copies ran while one was open for 0% of the time, Pallas kernels for 0%

profile of v3, /device:TPU:1, one launch (start us, length us, event | category | flops | bytes accessed | tf_op | source)
XLA Modules:
  0.0 177.5 jit_solution(14115318962672729435)
XLA Ops:
  0.6 0.7 convert_multiply_fusion
  1.3 0.9 multiply_convert_fusion.2
  2.3 16.7 %all_to_all.20.rest_0_ = bf16[8,128,256]{2,1,0:T(8,128)(2,1)S(1)} all-to-all(bf16[8,128,256]{2,1,0:T(8,128)(2,1)S(1)} %broadcast_in_dim.4), channel_id=1, replica_groups=mesh['y'=4,'xh'=2,'core'=2,'zh'=8,'zl'=2,'xl'=2] {'y','xh'}, dimensions={0} | all-to-all | bytes 1048576 | tf_op jit(solution)/shard_map/all_to_all | solution.py:140
  18.9 5.0 %collective-permute-start = (bf16[8,128,256]{2,1,0:T(8,128)(2,1)S(1)}, bf16[8,128,256]{2,1,0:T(8,128)(2,1)S(1)}, u32[]{:S(2)}, u32[]{:S(2)}) collective-permute-start(bf16[8,128,256]{2,1,0:T(8,128)(2,1)S(1)} %all_to_all.20.rest_0_), channel_id=1, source_target_pairs={{0,32},{32,0},{1,33},{33,1},{2,34},{34,2},{3,35},{35,3},{4,36},{36... | collective-permute-start | bytes 1572872 | tf_op jit(solution)/shard_map/ppermute | solution.py:144
  24.7 0.7 add_bitcast_fusion
  25.3 0.2 collective-permute-done.rest_1_
  25.5 4.7 %shard_map.104 = bf16[32,128,256]{2,1,0:T(8,128)(2,1)S(1)} custom-call(s32[1]{0:T(128)} %bitcast.12.count_ref, s32[96]{0:T(128)S(1)} %get-tuple-element.11.src_ref.dst_ref, s32[96]{0:T(128)S(1)} %get-tuple-element.10.dst_ref, bf16[96,128,128]{2,1,0:T(8,128)(2,1)} %bitcast.14, bf16[8,128,256]{2,1,0:T(8,128)(2,1)S(1)} %all_to_all.20.rest_0_, ...), custom_call_target="tpu_custom_call" | custom-call | flops 805306368 | bytes 3145728 | tf_op jit(solution)/shard_map/pallas_call | solution.py:89
  30.2 27.6 %all_to_all.21 = bf16[32,128,256]{2,1,0:T(8,128)(2,1)S(1)} all-to-all(bf16[32,128,256]{2,1,0:T(8,128)(2,1)S(1)} %shard_map.104), channel_id=1, replica_groups=mesh['y'=4,'xh'=2,'core'=2,'zh'=8,'zl'=2,'xl'=2] {'zl','xl'}, dimensions={0} | all-to-all | bytes 4194304 | tf_op jit(solution)/shard_map/all_to_all | solution.py:140
  57.8 0.0 copy-start
  57.8 0.0 copy-start.1
  57.8 1.2 reduce_sum.21
  59.1 14.4 %all-to-all-start.2 = ((bf16[8,128,256]{2,1,0:T(8,128)(2,1)}), bf16[8,128,256]{2,1,0:T(8,128)(2,1)S(1)}, u32[]{:S(2)}, u32[]{:S(2)}) async-start(bf16[8,128,256]{2,1,0:T(8,128)(2,1)} %reduce_sum.21), calls=%async_computation.2 | async-start | bytes 1048576 | tf_op jit(solution)/shard_map/all_to_all | solution.py:140
  73.4 0.1 copy.13.norm_ref
  73.6 25.2 %all-to-all-done.2.parts_ref = bf16[8,128,256]{2,1,0:T(8,128)(2,1)S(1)} async-done(((bf16[8,128,256]{2,1,0:T(8,128)(2,1)}), bf16[8,128,256]{2,1,0:T(8,128)(2,1)S(1)}, u32[]{:S(2)}, u32[]{:S(2)}) %all-to-all-start.2) | async-done | bytes 524320 | tf_op jit(solution)/shard_map/all_to_all | solution.py:140
  98.8 0.0 copy-done
  98.8 0.0 copy-done.1
  98.8 0.9 shard_map.105
  99.6 7.3 %collective-permute-start.1 = (f16[136,256]{1,0:T(8,128)(2,1)S(1)}, f16[136,256]{1,0:T(8,128)(2,1)S(1)}, u32[]{:S(2)}, u32[]{:S(2)}) collective-permute-start(f16[136,256]{1,0:T(8,128)(2,1)S(1)} %convert_element_type.41), channel_id=1, source_target_pairs={{0,1},{1,0},{2,3},{3,2},{4,5},{5,4},{6,7},{7,6},{8,9},{9,8},{10,11... | collective-permute-start | bytes 208904 | tf_op jit(solution)/shard_map/ppermute | solution.py:149
  106.9 1.7 collective-permute-done.1
  108.7 37.8 %all-gather.1 = f16[4352,256]{1,0:T(8,128)(2,1)S(1)} all-gather(f16[272,256]{1,0:T(8,128)(2,1)S(1)} %pad_maximum_fusion), channel_id=1, replica_groups=mesh['y'=4,'xh'=2,'core'=2,'zh'=8,'zl'=2,'xl'=2] {'zh','zl'}, dimensions={0}, use_global_device_ids=true | all-gather | bytes 2367488 | tf_op jit(solution)/shard_map/all_gather | solution.py:150
  146.4 0.3 fusion.3
  146.7 0.9 multiply_convert_fusion.rest_0_
  147.7 4.4 %shard_map.106 = bf16[16,128,256]{2,1,0:T(8,128)(2,1)S(1)} custom-call(s32[1]{0:T(128)} %bitcast.13.count_ref, s32[96]{0:T(128)S(1)} %get-tuple-element.9.src_ref, s32[96]{0:T(128)S(1)} %get-tuple-element.11.src_ref.dst_ref, bf16[96,128,128]{2,1,0:T(8,128)(2,1)} %bitcast.15, bf16[32,128,256]{2,1,0:T(8,128)(2,1)S(1)} %multiply_convert_fusion.rest_0_), custom_call_target="tpu_custom_call" | custom-call | flops 805306368 | bytes 3145728 | tf_op jit(solution)/shard_map/pallas_call | solution.py:89
  152.1 9.6 %collective-permute-start.2 = (bf16[8,128,256]{2,1,0:T(8,128)(2,1)S(1)}, bf16[8,128,256]{2,1,0:T(8,128)(2,1)S(1)}, u32[]{:S(2)}, u32[]{:S(2)}) collective-permute-start(bf16[8,128,256]{2,1,0:T(8,128)(2,1)S(1)} %slice.19), channel_id=1, source_target_pairs={{0,32},{32,0},{1,33},{33,1},{2,34},{34,2},{3,35},{35,3},{4,36},{36... | collective-permute-start | bytes 1572872 | tf_op jit(solution)/shard_map/ppermute | solution.py:144
  161.7 1.5 collective-permute-done.2
  163.2 0.1 add_convert_fusion
  163.3 13.3 %all_to_all.22 = bf16[8,128,256]{2,1,0:T(8,128)(2,1)S(1)} all-to-all(bf16[8,128,256]{2,1,0:T(8,128)(2,1)S(1)} %add_convert_fusion), channel_id=1, replica_groups=mesh['y'=4,'xh'=2,'core'=2,'zh'=8,'zl'=2,'xl'=2] {'y','xh'}, dimensions={0} | all-to-all | bytes 1048576 | tf_op jit(solution)/shard_map/all_to_all | solution.py:140
  176.7 0.1 convert_reduce_fusion
  176.7 0.7 multiply_convert_fusion.1
  (4 shorter events, 0.1 us)
Async XLA Ops:
  18.9 6.6 %collective-permute-start = (bf16[8,128,256]{2,1,0:T(8,128)(2,1)S(1)}, bf16[8,128,256]{2,1,0:T(8,128)(2,1)S(1)}, u32[]{:S(2)}, u32[]{:S(2)}) collective-permute-start(bf16[8,128,256]{2,1,0:T(8,128)(2,1)S(1)} %all_to_all.20.rest_0_), channel_id=1, source_target_pairs={{0,32},{32,0},{1,33},{33,1},{2,34},{34,2},{3,35},{35,3},{4,36},{36... | collective-permute-start | bytes 1572872 | tf_op jit(solution)/shard_map/ppermute | solution.py:144
  57.8 40.9 %copy-start = (bf16[256,256]{1,0:T(8,128)(2,1)S(1)}, bf16[256,256]{1,0:T(8,128)(2,1)}, u32[]{:S(2)}) copy-start(bf16[256,256]{1,0:T(8,128)(2,1)} %weight_ref.1) | copy-start | bytes 393220
  57.8 40.9 %copy-start.1 = (bf16[128,256]{1,0:T(8,128)(2,1)S(1)}, bf16[128,256]{1,0:T(8,128)(2,1)}, u32[]{:S(2)}) copy-start(bf16[128,256]{1,0:T(8,128)(2,1)} %cotangent_ref.1) | copy-start | bytes 196612
  59.1 39.7 %all-to-all-start.2 = ((bf16[8,128,256]{2,1,0:T(8,128)(2,1)}), bf16[8,128,256]{2,1,0:T(8,128)(2,1)S(1)}, u32[]{:S(2)}, u32[]{:S(2)}) async-start(bf16[8,128,256]{2,1,0:T(8,128)(2,1)} %reduce_sum.21), calls=%async_computation.2 | async-start | bytes 1048576 | tf_op jit(solution)/shard_map/all_to_all | solution.py:140
  99.6 9.0 %collective-permute-start.1 = (f16[136,256]{1,0:T(8,128)(2,1)S(1)}, f16[136,256]{1,0:T(8,128)(2,1)S(1)}, u32[]{:S(2)}, u32[]{:S(2)}) collective-permute-start(f16[136,256]{1,0:T(8,128)(2,1)S(1)} %convert_element_type.41), channel_id=1, source_target_pairs={{0,1},{1,0},{2,3},{3,2},{4,5},{5,4},{6,7},{7,6},{8,9},{9,8},{10,11... | collective-permute-start | bytes 208904 | tf_op jit(solution)/shard_map/ppermute | solution.py:149
  152.1 11.1 %collective-permute-start.2 = (bf16[8,128,256]{2,1,0:T(8,128)(2,1)S(1)}, bf16[8,128,256]{2,1,0:T(8,128)(2,1)S(1)}, u32[]{:S(2)}, u32[]{:S(2)}) collective-permute-start(bf16[8,128,256]{2,1,0:T(8,128)(2,1)S(1)} %slice.19), channel_id=1, source_target_pairs={{0,32},{32,0},{1,33},{33,1},{2,34},{34,2},{3,35},{35,3},{4,36},{36... | collective-permute-start | bytes 1572872 | tf_op jit(solution)/shard_map/ppermute | solution.py:144

commit v4 on v3

--- a/solution.py
+++ b/solution.py
@@ -10,9 +10,9 @@
 HID = 256
 BSZ = 128
 QDEN = 192
-GROUP = 16
+GROUP = 32
 AHEAD = 1
-CHUNK = 16
+CHUNK = 32
 
 NAMES = ("y", "xh", "core", "zh", "zl", "xl")
 BLK = ("y", "xh", "core")
@@ -104,9 +104,34 @@
     )(count, src, dst, edges, *tables)
 
 
-def middle_kernel(parts_ref, norm_ref, weight_ref, cotangent_ref, activated_ref, back_ref):
+def per_row(row):
+    square = jnp.broadcast_to(row, (BSZ, BSZ)).T
+    return jnp.concatenate([square] * (HID // BSZ), axis=1)
+
+
+def norm_of(counts_ref):
+    return counts_ref[...].astype(jnp.float32) / QDEN
+
+
+def end_kernel(parts_ref, counts_ref, out_ref):
     total = jnp.sum(parts_ref[...].astype(jnp.float32), axis=0)
-    norm = norm_ref[...]
+    out_ref[...] = (total * per_row(norm_of(counts_ref))).astype(jnp.bfloat16)
+
+
+def small_call(kernel, out_shape, *operands):
+    vmem = pl.BlockSpec(memory_space=pltpu.VMEM)
+    return pl.pallas_call(
+        kernel,
+        out_shape=out_shape,
+        in_specs=[vmem] * len(operands),
+        out_specs=jax.tree.map(lambda _: vmem, out_shape),
+        compiler_params=pltpu.CompilerParams(vmem_limit_bytes=12 * 1024 * 1024),
+    )(*operands)
+
+
+def middle_kernel(parts_ref, counts_ref, weight_ref, cotangent_ref, activated_ref, back_ref):
+    total = jnp.sum(parts_ref[...].astype(jnp.float32), axis=0)
+    norm = per_row(norm_of(counts_ref))
     aggregated = (total * norm).astype(jnp.bfloat16)
     weight = weight_ref[...]
     preact = jnp.dot(aggregated, weight, preferred_element_type=jnp.float32)
@@ -122,20 +147,6 @@
     back_ref[BSZ:] = jnp.broadcast_to(power, (8, HID))
 
 
-def middle(parts, norm, weight, cotangent):
-    vmem = pl.BlockSpec(memory_space=pltpu.VMEM)
-    return pl.pallas_call(
-        middle_kernel,
-        out_shape=(
-            jax.ShapeDtypeStruct(cotangent.shape, jnp.bfloat16),
-            jax.ShapeDtypeStruct((BSZ + 8, HID), jnp.float32),
-        ),
-        in_specs=[vmem] * 4,
-        out_specs=(vmem, vmem),
-        compiler_params=pltpu.CompilerParams(vmem_limit_bytes=12 * 1024 * 1024),
-    )(parts, norm, weight, cotangent)
-
-
 def exchange(value, axes):
     return lax.all_to_all(value, axes, 0, 0, tiled=True)
 
@@ -160,9 +171,7 @@
     hidden_values, node_scale, node_weight, weight, cotangent, block_rows, block_cols, block_count, edge_counts
 ):
     core = lax.axis_index("core")
-    node_norm = node_weight.astype(jnp.float32) / QDEN
-    norm = node_norm[:, None]
-    scaled = (hidden_values.astype(jnp.float32) * (node_scale * node_norm)[:, None]).astype(jnp.bfloat16)
+    counts = node_weight[None, :]
     edges = edge_counts[0, 0]
     rows = block_rows[0, 0]
     cols = block_cols[0, 0]
@@ -171,20 +180,24 @@
     row_to = (rows & ~1) + ((rows & 1) ^ lax.axis_index("xl"))
     col_at = ((cols & 1) ^ core) * 8 + (cols >> 1)
 
+    factor = node_scale * (node_weight.astype(jnp.float32) / QDEN)
+    scaled = (hidden_values.astype(jnp.float32) * factor[:, None]).astype(jnp.bfloat16)
     mine = exchange(jnp.broadcast_to(scaled[None], (8, BSZ, HID)), ("y", "xh"))
     theirs = other_core(mine)
     partial = spmm(True, count, col_at, row_at, edges, mine, theirs, 32)
     near = exchange(partial, ("zl", "xl"))
     near = add_up(near.reshape(4, 8, BSZ, HID)).astype(jnp.bfloat16)
     far = exchange(near, ("zh",))
-    activated, back = middle(far, norm, weight, cotangent)
+    own = jax.ShapeDtypeStruct((BSZ, HID), jnp.bfloat16)
+    sent = jax.ShapeDtypeStruct((BSZ + 8, HID), jnp.float32)
+    activated, back = small_call(middle_kernel, (own, sent), far, counts, weight, cotangent)
 
     table = gather_scaled(back)
     partial = spmm(False, count, row_to, col_at, edges, table, None, 16)
     received = other_core(partial[8:])
     pair = (partial[:8].astype(jnp.float32) + received.astype(jnp.float32)).astype(jnp.bfloat16)
     pair = exchange(pair, ("y", "xh"))
-    grad_hidden = (add_up(pair) * norm).astype(jnp.bfloat16)
+    grad_hidden = small_call(end_kernel, own, pair, counts)
     return activated, grad_hidden
 
 

time: 178 us -> 180 us (1.011)
  blocking collectives: 95.4 us -> 137 us
  waiting for transfers between devices: 28.6 us -> 3.38 us
  starting transfers between devices: 36.3 us -> 25.6 us
  Pallas kernels: 9.9 us -> 7.03 us
    all_to_all x3 -> x4, blocking collectives: 57.6 us -> 96.1 us  [exchange(): return lax.all_to_all(value, axes, 0, 0, tiled=True)]
    all_to_all x1 -> x0, waiting for transfers between devices: 25.2 us -> none  [exchange(): return lax.all_to_all(value, axes, 0, 0, tiled=True)]
    all_to_all x1 -> x0, starting transfers between devices: 14.4 us -> none  [exchange(): return lax.all_to_all(value, axes, 0, 0, tiled=True)]
    all_gather x1, blocking collectives: 37.8 us -> 41.4 us  [gather_scaled(): lax.all_gather(pair, ('zh', 'zl'), axis=0, tiled=True)]
    pallas_call x2, Pallas kernels: 9.04 us -> 5.42 us  [spmm(): pl.pallas_call(body, out_shape=jax.ShapeDtypeStruct((blocks, BSZ, HID), j...]
    ppermute x2, starting transfers between devices: 14.6 us -> 17.2 us  [other_core(): return lax.ppermute(value, 'core', [(0, 1), (1, 0)])]
  transfers between devices with their start and end apart: 4 -> 3, of which waited for: 4 -> 3; matrix products, arithmetic and copies ran while one was open for 0% -> 0% of each run, Pallas kernels for 0% -> 0%
where the time goes in v4:
time: 180 us; the launch traced here: 179 us
  blocking collectives  137 us (76%)
  starting transfers between devices  25.6 us (14%)
  Pallas kernels  7.03 us (4%)
  other arithmetic  4.09 us (2%)
  waiting for transfers between devices  3.38 us (2%)
    all_to_all x4, blocking collectives, exchange(): return lax.all_to_all(value, axes, 0, 0, tiled=True)  96.1 us
    all_gather x1, blocking collectives, gather_scaled(): lax.all_gather(pair, ('zh', 'zl'), axis=0, tiled=True)  41.4 us
    ppermute x2, starting transfers between devices, other_core(): return lax.ppermute(value, 'core', [(0, 1), (1, 0)])  17.2 us
    ppermute x1, starting transfers between devices, gather_scaled(): lax.ppermute(sent, 'xl', [(0, 1), (1, 0)])  8.47 us
    pallas_call x2, Pallas kernels, spmm(): pl.pallas_call(body, out_shape=jax.ShapeDtypeStruct((blocks, BSZ, HID), j...  5.42 us
  transfers between devices with their start and end apart: 3, of which 3 were waited for; matrix products, arithmetic and copies ran while one was open for 0% of the time, Pallas kernels for 0%

profile of v4, /device:TPU:1, one launch (start us, length us, event | category | flops | bytes accessed | tf_op | source)
XLA Modules:
  0.0 179.0 jit_solution(15620415805062023155)
XLA Ops:
  0.6 0.7 multiply_multiply_fusion
  1.3 0.9 multiply_convert_fusion.1
  2.3 16.7 %all_to_all.20.rest_0_ = bf16[8,128,256]{2,1,0:T(8,128)(2,1)S(1)} all-to-all(bf16[8,128,256]{2,1,0:T(8,128)(2,1)S(1)} %broadcast_in_dim.4), channel_id=1, replica_groups=mesh['y'=4,'xh'=2,'core'=2,'zh'=8,'zl'=2,'xl'=2] {'y','xh'}, dimensions={0} | all-to-all | bytes 1048576 | tf_op jit(solution)/shard_map/all_to_all | solution.py:151
  18.9 5.0 %collective-permute-start = (bf16[8,128,256]{2,1,0:T(8,128)(2,1)S(1)}, bf16[8,128,256]{2,1,0:T(8,128)(2,1)S(1)}, u32[]{:S(2)}, u32[]{:S(2)}) collective-permute-start(bf16[8,128,256]{2,1,0:T(8,128)(2,1)S(1)} %all_to_all.20.rest_0_), channel_id=1, source_target_pairs={{0,32},{32,0},{1,33},{33,1},{2,34},{34,2},{3,35},{35,3},{4,36},{36... | collective-permute-start | bytes 1572872 | tf_op jit(solution)/shard_map/ppermute | solution.py:155
  24.7 0.7 add_bitcast_fusion
  25.3 0.2 collective-permute-done.rest_1_
  25.5 2.7 %shard_map.104 = bf16[32,128,256]{2,1,0:T(8,128)(2,1)S(1)} custom-call(s32[1]{0:T(128)} %bitcast.11.count_ref, s32[96]{0:T(128)S(1)} %get-tuple-element.8.src_ref.dst_ref, s32[96]{0:T(128)S(1)} %get-tuple-element.7.dst_ref, bf16[96,128,128]{2,1,0:T(8,128)(2,1)} %bitcast.15, bf16[8,128,256]{2,1,0:T(8,128)(2,1)S(1)} %all_to_all.20.rest_0_, ...), custom_call_target="tpu_custom_call" | custom-call | flops 805306368 | bytes 3145728 | tf_op jit(solution)/shard_map/pallas_call | solution.py:89
  28.3 27.7 %all_to_all.21 = bf16[32,128,256]{2,1,0:T(8,128)(2,1)S(1)} all-to-all(bf16[32,128,256]{2,1,0:T(8,128)(2,1)S(1)} %shard_map.104), channel_id=1, replica_groups=mesh['y'=4,'xh'=2,'core'=2,'zh'=8,'zl'=2,'xl'=2] {'zl','xl'}, dimensions={0} | all-to-all | bytes 4194304 | tf_op jit(solution)/shard_map/all_to_all | solution.py:151
  55.9 0.0 copy-start
  55.9 0.0 copy-start.1
  56.0 0.0 copy-start.2
  56.0 0.4 reduce_sum.12
  56.3 38.0 %all_to_all.22.parts_ref = bf16[8,128,256]{2,1,0:T(8,128)(2,1)S(1)} all-to-all(bf16[8,128,256]{2,1,0:T(8,128)(2,1)S(1)} %reduce_sum.12), channel_id=1, replica_groups=mesh['y'=4,'xh'=2,'core'=2,'zh'=8,'zl'=2,'xl'=2] {'zh'}, dimensions={0} | all-to-all | bytes 1048576 | tf_op jit(solution)/shard_map/all_to_all | solution.py:151
  94.3 0.0 copy-done
  94.3 0.0 copy-done.1
  94.3 0.0 copy-done.2
  94.3 0.9 shard_map.105
  95.2 8.5 %collective-permute-start.1 = (f16[136,256]{1,0:T(8,128)(2,1)S(1)}, f16[136,256]{1,0:T(8,128)(2,1)S(1)}, u32[]{:S(2)}, u32[]{:S(2)}) collective-permute-start(f16[136,256]{1,0:T(8,128)(2,1)S(1)} %convert_element_type.35), channel_id=1, source_target_pairs={{0,1},{1,0},{2,3},{3,2},{4,5},{5,4},{6,7},{7,6},{8,9},{9,8},{10,11... | collective-permute-start | bytes 208904 | tf_op jit(solution)/shard_map/ppermute | solution.py:160
  103.7 1.7 collective-permute-done.1
  105.4 41.4 %all-gather.1 = f16[4352,256]{1,0:T(8,128)(2,1)S(1)} all-gather(f16[272,256]{1,0:T(8,128)(2,1)S(1)} %pad_maximum_fusion), channel_id=1, replica_groups=mesh['y'=4,'xh'=2,'core'=2,'zh'=8,'zl'=2,'xl'=2] {'zh','zl'}, dimensions={0}, use_global_device_ids=true | all-gather | bytes 2367488 | tf_op jit(solution)/shard_map/all_gather | solution.py:161
  146.8 0.3 fusion.3
  147.1 0.9 multiply_convert_fusion.rest_0_
  148.0 2.7 %shard_map.106 = bf16[16,128,256]{2,1,0:T(8,128)(2,1)S(1)} custom-call(s32[1]{0:T(128)} %bitcast.12.count_ref, s32[96]{0:T(128)S(1)} %get-tuple-element.6.src_ref, s32[96]{0:T(128)S(1)} %get-tuple-element.8.src_ref.dst_ref, bf16[96,128,128]{2,1,0:T(8,128)(2,1)} %bitcast.16, bf16[32,128,256]{2,1,0:T(8,128)(2,1)S(1)} %multiply_convert_fusion.rest_0_), custom_call_target="tpu_custom_call" | custom-call | flops 805306368 | bytes 3145728 | tf_op jit(solution)/shard_map/pallas_call | solution.py:89
  150.8 12.1 %collective-permute-start.2 = (bf16[8,128,256]{2,1,0:T(8,128)(2,1)S(1)}, bf16[8,128,256]{2,1,0:T(8,128)(2,1)S(1)}, u32[]{:S(2)}, u32[]{:S(2)}) collective-permute-start(bf16[8,128,256]{2,1,0:T(8,128)(2,1)S(1)} %slice.19), channel_id=1, source_target_pairs={{0,32},{32,0},{1,33},{33,1},{2,34},{34,2},{3,35},{35,3},{4,36},{36... | collective-permute-start | bytes 1572872 | tf_op jit(solution)/shard_map/ppermute | solution.py:155
  162.9 1.5 collective-permute-done.2
  164.4 0.1 add_convert_fusion
  164.6 13.8 %all_to_all.23.parts_ref = bf16[8,128,256]{2,1,0:T(8,128)(2,1)S(1)} all-to-all(bf16[8,128,256]{2,1,0:T(8,128)(2,1)S(1)} %add_convert_fusion), channel_id=1, replica_groups=mesh['y'=4,'xh'=2,'core'=2,'zh'=8,'zl'=2,'xl'=2] {'y','xh'}, dimensions={0} | all-to-all | bytes 1048576 | tf_op jit(solution)/shard_map/all_to_all | solution.py:151
  178.3 0.7 shard_map.107
  (4 shorter events, 0.1 us)
Async XLA Ops:
  18.9 6.6 %collective-permute-start = (bf16[8,128,256]{2,1,0:T(8,128)(2,1)S(1)}, bf16[8,128,256]{2,1,0:T(8,128)(2,1)S(1)}, u32[]{:S(2)}, u32[]{:S(2)}) collective-permute-start(bf16[8,128,256]{2,1,0:T(8,128)(2,1)S(1)} %all_to_all.20.rest_0_), channel_id=1, source_target_pairs={{0,32},{32,0},{1,33},{33,1},{2,34},{34,2},{3,35},{35,3},{4,36},{36... | collective-permute-start | bytes 1572872 | tf_op jit(solution)/shard_map/ppermute | solution.py:155
  55.9 38.4 %copy-start = (bf16[256,256]{1,0:T(8,128)(2,1)S(1)}, bf16[256,256]{1,0:T(8,128)(2,1)}, u32[]{:S(2)}) copy-start(bf16[256,256]{1,0:T(8,128)(2,1)} %weight_ref.1) | copy-start | bytes 393220
  55.9 38.4 %copy-start.1 = (bf16[128,256]{1,0:T(8,128)(2,1)S(1)}, bf16[128,256]{1,0:T(8,128)(2,1)}, u32[]{:S(2)}) copy-start(bf16[128,256]{1,0:T(8,128)(2,1)} %cotangent_ref.1) | copy-start | bytes 196612
  56.0 38.4 %copy-start.2 = (s32[128]{0:T(128)S(1)}, s32[128]{0:T(128)}, u32[]{:S(2)}) copy-start(s32[128]{0:T(128)} %param.11) | copy-start | bytes 1540
  95.2 10.2 %collective-permute-start.1 = (f16[136,256]{1,0:T(8,128)(2,1)S(1)}, f16[136,256]{1,0:T(8,128)(2,1)S(1)}, u32[]{:S(2)}, u32[]{:S(2)}) collective-permute-start(f16[136,256]{1,0:T(8,128)(2,1)S(1)} %convert_element_type.35), channel_id=1, source_target_pairs={{0,1},{1,0},{2,3},{3,2},{4,5},{5,4},{6,7},{7,6},{8,9},{9,8},{10,11... | collective-permute-start | bytes 208904 | tf_op jit(solution)/shard_map/ppermute | solution.py:160
  150.8 13.6 %collective-permute-start.2 = (bf16[8,128,256]{2,1,0:T(8,128)(2,1)S(1)}, bf16[8,128,256]{2,1,0:T(8,128)(2,1)S(1)}, u32[]{:S(2)}, u32[]{:S(2)}) collective-permute-start(bf16[8,128,256]{2,1,0:T(8,128)(2,1)S(1)} %slice.19), channel_id=1, source_target_pairs={{0,32},{32,0},{1,33},{33,1},{2,34},{34,2},{3,35},{35,3},{4,36},{36... | collective-permute-start | bytes 1572872 | tf_op jit(solution)/shard_map/ppermute | solution.py:155

commit v5 on v4

--- a/solution.py
+++ b/solution.py
@@ -13,6 +13,7 @@
 GROUP = 32
 AHEAD = 1
 CHUNK = 32
+SPREAD = 2 * BSZ + 16
 
 NAMES = ("y", "xh", "core", "zh", "zl", "xl")
 BLK = ("y", "xh", "core")
@@ -25,7 +26,7 @@
     slots = edge_buf.shape[0]
     count = count_ref[0]
     half = first_ref.shape[0]
-    blocks = out_ref.shape[0]
+    blocks = acc.shape[0] - 1
     for c in range(slots // CHUNK):
 
         @pl.when(c * CHUNK < count)
@@ -68,10 +69,17 @@
 
             lax.fori_loop(0, CHUNK // GROUP, step, 0)
 
-    out_ref[...] = acc[:blocks].astype(jnp.bfloat16)
-
-
-def spmm(transposed, count, src, dst, edges, first, second, blocks):
+    if len(out_ref.shape) == 3:
+        out_ref[...] = acc[:blocks].astype(jnp.bfloat16)
+    else:
+        for z in range(blocks // 2):
+            for h in range(2):
+                out_ref[pl.ds(SPREAD * z + BSZ * h, BSZ)] = acc[2 * z + h].astype(jnp.bfloat16)
+            if z < blocks // 2 - 1:
+                out_ref[pl.ds(SPREAD * z + 2 * BSZ, 16)] = jnp.zeros((16, HID), jnp.bfloat16)
+
+
+def spmm(transposed, count, src, dst, edges, first, second, blocks, out_shape):
     slots = edges.shape[0]
     vmem = pl.BlockSpec(memory_space=pltpu.VMEM)
     smem = pl.BlockSpec(memory_space=pltpu.SMEM)
@@ -88,7 +96,7 @@
     table_rows = 1 if second is None else 2 * first.shape[0]
     return pl.pallas_call(
         body,
-        out_shape=jax.ShapeDtypeStruct((blocks, BSZ, HID), jnp.bfloat16),
+        out_shape=jax.ShapeDtypeStruct(out_shape, jnp.bfloat16),
         in_specs=[smem, smem, smem, pl.BlockSpec(memory_space=pl.ANY)] + [vmem] * len(tables),
         out_specs=vmem,
         scratch_shapes=[
@@ -129,8 +137,8 @@
     )(*operands)
 
 
-def middle_kernel(parts_ref, counts_ref, weight_ref, cotangent_ref, activated_ref, back_ref):
-    total = jnp.sum(parts_ref[...].astype(jnp.float32), axis=0)
+def middle_kernel(mine_ref, theirs_ref, counts_ref, weight_ref, cotangent_ref, activated_ref, back_ref):
+    total = mine_ref[...].astype(jnp.float32) + theirs_ref[...].astype(jnp.float32)
     norm = per_row(norm_of(counts_ref))
     aggregated = (total * norm).astype(jnp.bfloat16)
     weight = weight_ref[...]
@@ -157,14 +165,20 @@
 
 def gather_scaled(value):
     sent = value.astype(jnp.float16)
-    pair = jnp.concatenate([sent, lax.ppermute(sent, "xl", [(0, 1), (1, 0)])], axis=0)
+    pair = jnp.concatenate([sent, other_x(sent)], axis=0)
     pairs = lax.all_gather(pair, ("zh", "zl"), axis=0, tiled=True).reshape(32, BSZ + 8, HID)
     back = jnp.exp2(-pairs[:, BSZ : BSZ + 1, :1].astype(jnp.float32))
     return (pairs[:, :BSZ].astype(jnp.float32) * back).astype(jnp.bfloat16)
 
 
-def add_up(value):
-    return jnp.sum(value.astype(jnp.float32), axis=0)
+def other_x(value):
+    return lax.ppermute(value, "xl", [(0, 1), (1, 0)])
+
+
+def summed_over_z(partial):
+    shard = lax.psum_scatter(partial, ("zh", "zl"), scatter_dimension=0, tiled=True)
+    shard = lax.optimization_barrier(shard)
+    return lax.dynamic_slice(shard, (lax.axis_index(("zh", "zl")), 0), (2 * BSZ, HID))
 
 
 def per_device(
@@ -176,24 +190,22 @@
     rows = block_rows[0, 0]
     cols = block_cols[0, 0]
     count = block_count[0]
-    row_at = (rows & 3) * 8 + (rows >> 2)
-    row_to = (rows & ~1) + ((rows & 1) ^ lax.axis_index("xl"))
+    row_at = (rows & ~1) + ((rows & 1) ^ lax.axis_index("xl"))
     col_at = ((cols & 1) ^ core) * 8 + (cols >> 1)
 
     factor = node_scale * (node_weight.astype(jnp.float32) / QDEN)
     scaled = (hidden_values.astype(jnp.float32) * factor[:, None]).astype(jnp.bfloat16)
     mine = exchange(jnp.broadcast_to(scaled[None], (8, BSZ, HID)), ("y", "xh"))
     theirs = other_core(mine)
-    partial = spmm(True, count, col_at, row_at, edges, mine, theirs, 32)
-    near = exchange(partial, ("zl", "xl"))
-    near = add_up(near.reshape(4, 8, BSZ, HID)).astype(jnp.bfloat16)
-    far = exchange(near, ("zh",))
+    partial = spmm(True, count, col_at, row_at, edges, mine, theirs, 32, (16 * (SPREAD - 1), HID))
+    sums = summed_over_z(partial)
+    received = other_x(sums[BSZ:])
     own = jax.ShapeDtypeStruct((BSZ, HID), jnp.bfloat16)
     sent = jax.ShapeDtypeStruct((BSZ + 8, HID), jnp.float32)
-    activated, back = small_call(middle_kernel, (own, sent), far, counts, weight, cotangent)
+    activated, back = small_call(middle_kernel, (own, sent), sums[:BSZ], received, counts, weight, cotangent)
 
     table = gather_scaled(back)
-    partial = spmm(False, count, row_to, col_at, edges, table, None, 16)
+    partial = spmm(False, count, row_at, col_at, edges, table, None, 16, (16, BSZ, HID))
     received = other_core(partial[8:])
     pair = (partial[:8].astype(jnp.float32) + received.astype(jnp.float32)).astype(jnp.bfloat16)
     pair = exchange(pair, ("y", "xh"))

time: 180 us -> 162 us (0.900)
  blocking collectives: 137 us -> 108 us
  starting transfers between devices: 25.6 us -> 31.2 us
  waiting for transfers between devices: 3.38 us -> 6.01 us
  local copies, waits for them, and re-layouts: 0.08 us -> 1.94 us
    all_to_all x4 -> x2, blocking collectives: 96.1 us -> 29.9 us  [exchange(): return lax.all_to_all(value, axes, 0, 0, tiled=True)]
    unnamed x0 -> x1, blocking collectives: none -> 40.5 us
    ppermute x2, starting transfers between devices: 17.2 us -> 20.9 us  [other_core(): return lax.ppermute(value, 'core', [(0, 1), (1, 0)])]
    all_gather x1, blocking collectives: 41.4 us -> 37.8 us  [gather_scaled(): lax.all_gather(pair, ('zh', 'zl'), axis=0, tiled=True)]
    ppermute x1 -> x2, waiting for transfers between devices: 1.68 us -> 4.31 us  [other_x(): return lax.ppermute(value, 'xl', [(0, 1), (1, 0)])]
    unnamed x6 -> x10, local copies, waits for them, and re-layouts: 0.01 us -> 1.83 us
    ppermute x1 -> x2, starting transfers between devices: 8.47 us -> 8.65 us  [other_x(): return lax.ppermute(value, 'xl', [(0, 1), (1, 0)])]
  transfers between devices with their start and end apart: 3 -> 5, of which waited for: 3 -> 4; matrix products, arithmetic and copies ran while one was open for 0% -> 1% of each run, Pallas kernels for 0% -> 0%
where the time goes in v5:
time: 162 us; the launch traced here: 160 us
  blocking collectives  108 us (67%)
  starting transfers between devices  31.2 us (19%)
  Pallas kernels  7.03 us (4%)
  waiting for transfers between devices  6.01 us (4%)
  other arithmetic  3.71 us (2%)
  between operations  2.12 us (1%)
  local copies, waits for them, and re-layouts  1.94 us (1%)
    unnamed x1, blocking collectives  40.5 us
    all_gather x1, blocking collectives, gather_scaled(): lax.all_gather(pair, ('zh', 'zl'), axis=0, tiled=True)  37.8 us
    all_to_all x2, blocking collectives, exchange(): return lax.all_to_all(value, axes, 0, 0, tiled=True)  29.9 us
    ppermute x2, starting transfers between devices, other_core(): return lax.ppermute(value, 'core', [(0, 1), (1, 0)])  20.9 us
    ppermute x2, starting transfers between devices, other_x(): return lax.ppermute(value, 'xl', [(0, 1), (1, 0)])  8.65 us
    pallas_call x2, Pallas kernels, spmm(): pl.pallas_call(body, out_shape=jax.ShapeDtypeStruct(out_shape, jnp.bfloat...  5.43 us
    ppermute x2, waiting for transfers between devices, other_x(): return lax.ppermute(value, 'xl', [(0, 1), (1, 0)])  4.31 us
  transfers between devices with their start and end apart: 5, of which 4 were waited for; matrix products, arithmetic and copies ran while one was open for 1% of the time, Pallas kernels for 0%

profile of v5, /device:TPU:1, one launch (start us, length us, event | category | flops | bytes accessed | tf_op | source)
XLA Modules:
  0.0 160.2 jit_solution(16957173109593095307)
XLA Ops:
  0.6 0.7 multiply_multiply_fusion
  1.3 0.9 multiply_convert_fusion.1
  2.3 16.7 %all_to_all.10.rest_0_ = bf16[8,128,256]{2,1,0:T(8,128)(2,1)S(1)} all-to-all(bf16[8,128,256]{2,1,0:T(8,128)(2,1)S(1)} %broadcast_in_dim.4), channel_id=1, replica_groups=mesh['y'=4,'xh'=2,'core'=2,'zh'=8,'zl'=2,'xl'=2] {'y','xh'}, dimensions={0} | all-to-all | bytes 1048576 | tf_op jit(solution)/shard_map/all_to_all | solution.py:159
  18.9 5.0 %collective-permute-start = (bf16[8,128,256]{2,1,0:T(8,128)(2,1)S(1)}, bf16[8,128,256]{2,1,0:T(8,128)(2,1)S(1)}, u32[]{:S(2)}, u32[]{:S(2)}) collective-permute-start(bf16[8,128,256]{2,1,0:T(8,128)(2,1)S(1)} %all_to_all.10.rest_0_), channel_id=1, source_target_pairs={{0,32},{32,0},{1,33},{33,1},{2,34},{34,2},{3,35},{35,3},{4,36},{36... | collective-permute-start | bytes 1572872 | tf_op jit(solution)/shard_map/ppermute | solution.py:163
  24.7 0.7 add_bitcast_fusion
  25.3 0.2 collective-permute-done.rest_1_
  25.5 2.8 %shard_map.104 = bf16[4336,256]{1,0:T(8,128)(2,1)S(1)} custom-call(s32[1]{0:T(128)} %bitcast.11.count_ref, s32[96]{0:T(128)S(1)} %get-tuple-element.9.src_ref.dst_ref, s32[96]{0:T(128)S(1)} %get-tuple-element.8.dst_ref.src_ref, bf16[96,128,128]{2,1,0:T(8,128)(2,1)} %bitcast.15, bf16[8,128,256]{2,1,0:T(8,128)(2,1)S(1)} %all_to_all.10.rest_0_, ...), custom_call_target="tpu_custom_call" | custom-call | flops 805306368 | bytes 3145728 | tf_op jit(solution)/shard_map/pallas_call | solution.py:97
  28.3 0.0 copy-start
  28.3 0.0 copy-start.1
  28.3 0.0 copy-start.2
  28.3 40.5 %fusion = bf16[272,256]{1,0:T(8,128)(2,1)S(1)} fusion(bf16[4336,256]{1,0:T(8,128)(2,1)S(1)} %shard_map.104), kind=kCustom, calls=%all-reduce-scatter | all-reduce-scatter fusion | flops 1114113 | bytes 2361344
  68.8 1.6 collective-permute-start.4
  70.4 1.3 dynamic-slice.6
  72.4 0.0 collective-permute-done.4
  72.4 0.5 concatenate.4
  73.0 5.3 %collective-permute-start.1 = (bf16[128,256]{1,0:T(8,128)(2,1)S(1)}, bf16[128,256]{1,0:T(8,128)(2,1)S(1)}, u32[]{:S(2)}, u32[]{:S(2)}) collective-permute-start(bf16[128,256]{1,0:T(8,128)(2,1)S(1)} %get-tuple-element.6), channel_id=1, source_target_pairs={{0,1},{1,0},{2,3},{3,2},{4,5},{5,4},{6,7},{7,6},{8,9},{9,8},{10,11... | collective-permute-start | bytes 196616 | tf_op jit(solution)/shard_map/ppermute | solution.py:175
  78.3 1.6 %collective-permute-done.1.theirs_ref = bf16[128,256]{1,0:T(8,128)(2,1)S(1)} collective-permute-done((bf16[128,256]{1,0:T(8,128)(2,1)S(1)}, bf16[128,256]{1,0:T(8,128)(2,1)S(1)}, u32[]{:S(2)}, u32[]{:S(2)}) %collective-permute-start.1) | collective-permute-done | bytes 65568 | tf_op jit(solution)/shard_map/ppermute | solution.py:175
  79.9 0.0 copy-done
  79.9 0.0 copy-done.1
  79.9 0.0 copy-done.2
  79.9 0.9 shard_map.105
  80.8 3.4 %collective-permute-start.2 = (f16[136,256]{1,0:T(8,128)(2,1)S(1)}, f16[136,256]{1,0:T(8,128)(2,1)S(1)}, u32[]{:S(2)}, u32[]{:S(2)}) collective-permute-start(f16[136,256]{1,0:T(8,128)(2,1)S(1)} %convert_element_type.33), channel_id=1, source_target_pairs={{0,1},{1,0},{2,3},{3,2},{4,5},{5,4},{6,7},{7,6},{8,9},{9,8},{10,11... | collective-permute-start | bytes 208904 | tf_op jit(solution)/shard_map/ppermute | solution.py:175
  84.2 2.7 %collective-permute-done.2 = f16[136,256]{1,0:T(8,128)(2,1)S(1)} collective-permute-done((f16[136,256]{1,0:T(8,128)(2,1)S(1)}, f16[136,256]{1,0:T(8,128)(2,1)S(1)}, u32[]{:S(2)}, u32[]{:S(2)}) %collective-permute-start.2) | collective-permute-done | bytes 69664 | tf_op jit(solution)/shard_map/ppermute | solution.py:175
  86.9 37.8 %all-gather.1 = f16[4352,256]{1,0:T(8,128)(2,1)S(1)} all-gather(f16[272,256]{1,0:T(8,128)(2,1)S(1)} %pad_maximum_fusion), channel_id=1, replica_groups=mesh['y'=4,'xh'=2,'core'=2,'zh'=8,'zl'=2,'xl'=2] {'zh','zl'}, dimensions={0}, use_global_device_ids=true | all-gather | bytes 2367488 | tf_op jit(solution)/shard_map/all_gather | solution.py:169
  124.7 0.3 fusion.4
  125.0 0.9 multiply_convert_fusion.rest_0_
  125.9 2.7 %shard_map.106 = bf16[16,128,256]{2,1,0:T(8,128)(2,1)S(1)} custom-call(s32[1]{0:T(128)} %bitcast.12.count_ref, s32[96]{0:T(128)S(1)} %get-tuple-element.8.dst_ref.src_ref, s32[96]{0:T(128)S(1)} %get-tuple-element.9.src_ref.dst_ref, bf16[96,128,128]{2,1,0:T(8,128)(2,1)} %bitcast.16, bf16[32,128,256]{2,1,0:T(8,128)(2,1)S(1)} %multiply_convert_fusion.rest_0_), custom_call_target="tpu_custom_call" | custom-call | flops 805306368 | bytes 3145728 | tf_op jit(solution)/shard_map/pallas_call | solution.py:97
  128.6 15.9 %collective-permute-start.3 = (bf16[8,128,256]{2,1,0:T(8,128)(2,1)S(1)}, bf16[8,128,256]{2,1,0:T(8,128)(2,1)S(1)}, u32[]{:S(2)}, u32[]{:S(2)}) collective-permute-start(bf16[8,128,256]{2,1,0:T(8,128)(2,1)S(1)} %slice.27), channel_id=1, source_target_pairs={{0,32},{32,0},{1,33},{33,1},{2,34},{34,2},{3,35},{35,3},{4,36},{36... | collective-permute-start | bytes 1572872 | tf_op jit(solution)/shard_map/ppermute | solution.py:163
  144.5 1.5 collective-permute-done.3
  146.0 0.1 add_convert_fusion
  146.2 13.2 %all_to_all.11.parts_ref = bf16[8,128,256]{2,1,0:T(8,128)(2,1)S(1)} all-to-all(bf16[8,128,256]{2,1,0:T(8,128)(2,1)S(1)} %add_convert_fusion), channel_id=1, replica_groups=mesh['y'=4,'xh'=2,'core'=2,'zh'=8,'zl'=2,'xl'=2] {'y','xh'}, dimensions={0} | all-to-all | bytes 1048576 | tf_op jit(solution)/shard_map/all_to_all | solution.py:159
  159.4 0.7 shard_map.107
  (7 shorter events, 0.2 us)
Async XLA Ops:
  18.9 6.6 %collective-permute-start = (bf16[8,128,256]{2,1,0:T(8,128)(2,1)S(1)}, bf16[8,128,256]{2,1,0:T(8,128)(2,1)S(1)}, u32[]{:S(2)}, u32[]{:S(2)}) collective-permute-start(bf16[8,128,256]{2,1,0:T(8,128)(2,1)S(1)} %all_to_all.10.rest_0_), channel_id=1, source_target_pairs={{0,32},{32,0},{1,33},{33,1},{2,34},{34,2},{3,35},{35,3},{4,36},{36... | collective-permute-start | bytes 1572872 | tf_op jit(solution)/shard_map/ppermute | solution.py:163
  28.3 51.6 %copy-start = (bf16[256,256]{1,0:T(8,128)(2,1)S(1)}, bf16[256,256]{1,0:T(8,128)(2,1)}, u32[]{:S(2)}) copy-start(bf16[256,256]{1,0:T(8,128)(2,1)} %weight_ref.1) | copy-start | bytes 393220
  28.3 51.6 %copy-start.1 = (bf16[128,256]{1,0:T(8,128)(2,1)S(1)}, bf16[128,256]{1,0:T(8,128)(2,1)}, u32[]{:S(2)}) copy-start(bf16[128,256]{1,0:T(8,128)(2,1)} %cotangent_ref.1) | copy-start | bytes 196612
  28.3 51.6 %copy-start.2 = (s32[128]{0:T(128)S(1)}, s32[128]{0:T(128)}, u32[]{:S(2)}) copy-start(s32[128]{0:T(128)} %param.11) | copy-start | bytes 1540
  68.8 3.5 %collective-permute-start.4 = (bf16[15,256]{1,0:T(8,128)(2,1)S(1)}, bf16[15,256]{1,0:T(8,128)(2,1)S(1)}, u32[]{:S(2)}, u32[]{:S(2)}) collective-permute-start(bf16[15,256]{1,0:T(8,128)(2,1)S(1)} %slice.28), channel_id=1, source_target_pairs={{0,2},{2,4},{4,6},{6,8},{8,10},{10,12},{12,14},{14,16},{16,18},{18... | collective-permute-start | bytes 23048
  73.0 6.9 %collective-permute-start.1 = (bf16[128,256]{1,0:T(8,128)(2,1)S(1)}, bf16[128,256]{1,0:T(8,128)(2,1)S(1)}, u32[]{:S(2)}, u32[]{:S(2)}) collective-permute-start(bf16[128,256]{1,0:T(8,128)(2,1)S(1)} %get-tuple-element.6), channel_id=1, source_target_pairs={{0,1},{1,0},{2,3},{3,2},{4,5},{5,4},{6,7},{7,6},{8,9},{9,8},{10,11... | collective-permute-start | bytes 196616 | tf_op jit(solution)/shard_map/ppermute | solution.py:175
  80.8 6.0 %collective-permute-start.2 = (f16[136,256]{1,0:T(8,128)(2,1)S(1)}, f16[136,256]{1,0:T(8,128)(2,1)S(1)}, u32[]{:S(2)}, u32[]{:S(2)}) collective-permute-start(f16[136,256]{1,0:T(8,128)(2,1)S(1)} %convert_element_type.33), channel_id=1, source_target_pairs={{0,1},{1,0},{2,3},{3,2},{4,5},{5,4},{6,7},{7,6},{8,9},{9,8},{10,11... | collective-permute-start | bytes 208904 | tf_op jit(solution)/shard_map/ppermute | solution.py:175
  128.6 17.4 %collective-permute-start.3 = (bf16[8,128,256]{2,1,0:T(8,128)(2,1)S(1)}, bf16[8,128,256]{2,1,0:T(8,128)(2,1)S(1)}, u32[]{:S(2)}, u32[]{:S(2)}) collective-permute-start(bf16[8,128,256]{2,1,0:T(8,128)(2,1)S(1)} %slice.27), channel_id=1, source_target_pairs={{0,32},{32,0},{1,33},{33,1},{2,34},{34,2},{3,35},{35,3},{4,36},{36... | collective-permute-start | bytes 1572872 | tf_op jit(solution)/shard_map/ppermute | solution.py:163

commit v6 on v5

--- a/solution.py
+++ b/solution.py
@@ -137,22 +137,36 @@
     )(*operands)
 
 
-def middle_kernel(mine_ref, theirs_ref, counts_ref, weight_ref, cotangent_ref, activated_ref, back_ref):
-    total = mine_ref[...].astype(jnp.float32) + theirs_ref[...].astype(jnp.float32)
-    norm = per_row(norm_of(counts_ref))
-    aggregated = (total * norm).astype(jnp.bfloat16)
+def middle_kernel(
+    sums_ref, received_ref, counts_ref, weight_ref, cotangent_ref, activated_ref, back_ref
+):
     weight = weight_ref[...]
-    preact = jnp.dot(aggregated, weight, preferred_element_type=jnp.float32)
-    gate = jax.nn.sigmoid(preact)
-    activated_ref[...] = (preact * gate).astype(jnp.bfloat16)
-    slope = gate * (1.0 + preact * (1.0 - gate))
-    dpre = (cotangent_ref[...].astype(jnp.float32) * slope).astype(jnp.bfloat16)
-    back = lax.dot_general(dpre, weight, (((1,), (1,)), ((), ())), preferred_element_type=jnp.float32)
-    back = (back * norm).astype(jnp.bfloat16).astype(jnp.float32)
-    largest = jnp.maximum(jnp.max(jnp.abs(back), axis=(0, 1), keepdims=True), 1e-30)
+    largest = jnp.full((1, 1), 1e-30, jnp.float32)
+    backs = []
+    for h in range(2):
+        mine = sums_ref[pl.ds(BSZ * h, BSZ)].astype(jnp.float32)
+        total = mine + received_ref[pl.ds(BSZ * (1 - h), BSZ)].astype(jnp.float32)
+        if h == 0:
+            norm = per_row(norm_of(counts_ref))
+            cotangent = cotangent_ref[...].astype(jnp.float32)
+        else:
+            norm = per_row(received_ref[pl.ds(3 * BSZ, 16)].astype(jnp.float32)[:1, :BSZ] / QDEN)
+            cotangent = received_ref[pl.ds(2 * BSZ, BSZ)].astype(jnp.float32)
+        aggregated = (total * norm).astype(jnp.bfloat16)
+        preact = jnp.dot(aggregated, weight, preferred_element_type=jnp.float32)
+        gate = jax.nn.sigmoid(preact)
+        if h == 0:
+            activated_ref[...] = (preact * gate).astype(jnp.bfloat16)
+        slope = gate * (1.0 + preact * (1.0 - gate))
+        dpre = (cotangent * slope).astype(jnp.bfloat16)
+        back = lax.dot_general(dpre, weight, (((1,), (1,)), ((), ())), preferred_element_type=jnp.float32)
+        back = (back * norm).astype(jnp.bfloat16).astype(jnp.float32)
+        largest = jnp.maximum(largest, jnp.max(jnp.abs(back), axis=(0, 1), keepdims=True))
+        backs.append(back)
     power = 14.0 - jnp.floor(jnp.log2(largest))
-    back_ref[:BSZ] = back * jnp.exp2(power)
-    back_ref[BSZ:] = jnp.broadcast_to(power, (8, HID))
+    for h in range(2):
+        back_ref[pl.ds(BSZ * h, BSZ)] = backs[h] * jnp.exp2(power)
+    back_ref[pl.ds(2 * BSZ, 8)] = jnp.broadcast_to(power, (8, HID))
 
 
 def exchange(value, axes):
@@ -165,10 +179,10 @@
 
 def gather_scaled(value):
     sent = value.astype(jnp.float16)
-    pair = jnp.concatenate([sent, other_x(sent)], axis=0)
-    pairs = lax.all_gather(pair, ("zh", "zl"), axis=0, tiled=True).reshape(32, BSZ + 8, HID)
-    back = jnp.exp2(-pairs[:, BSZ : BSZ + 1, :1].astype(jnp.float32))
-    return (pairs[:, :BSZ].astype(jnp.float32) * back).astype(jnp.bfloat16)
+    pairs = lax.all_gather(sent, ("zh", "zl"), axis=0, tiled=True).reshape(16, 2 * BSZ + 8, HID)
+    back = jnp.exp2(-pairs[:, 2 * BSZ : 2 * BSZ + 1, :1].astype(jnp.float32))
+    table = (pairs[:, : 2 * BSZ].astype(jnp.float32) * back).astype(jnp.bfloat16)
+    return table.reshape(32, BSZ, HID)
 
 
 def other_x(value):
@@ -199,10 +213,11 @@
     theirs = other_core(mine)
     partial = spmm(True, count, col_at, row_at, edges, mine, theirs, 32, (16 * (SPREAD - 1), HID))
     sums = summed_over_z(partial)
-    received = other_x(sums[BSZ:])
+    small = jnp.broadcast_to(jnp.tile(node_weight.astype(jnp.bfloat16), HID // BSZ), (16, HID))
+    received = other_x(jnp.concatenate([sums, cotangent, small], axis=0))
     own = jax.ShapeDtypeStruct((BSZ, HID), jnp.bfloat16)
-    sent = jax.ShapeDtypeStruct((BSZ + 8, HID), jnp.float32)
-    activated, back = small_call(middle_kernel, (own, sent), sums[:BSZ], received, counts, weight, cotangent)
+    sent = jax.ShapeDtypeStruct((2 * BSZ + 8, HID), jnp.float32)
+    activated, back = small_call(middle_kernel, (own, sent), sums, received, counts, weight, cotangent)
 
     table = gather_scaled(back)
     partial = spmm(False, count, row_at, col_at, edges, table, None, 16, (16, BSZ, HID))

time: 162 us -> 157 us (0.969)
  starting transfers between devices: 31.2 us -> 24.4 us
    ppermute x2 -> x1, starting transfers between devices: 8.65 us -> 2.2 us  [other_x(): return lax.ppermute(value, 'xl', [(0, 1), (1, 0)])]
    ppermute x2 -> x1, waiting for transfers between devices: 4.31 us -> 4.3 us  [other_x(): return lax.ppermute(value, 'xl', [(0, 1), (1, 0)])]
  transfers between devices with their start and end apart: 5 -> 4, of which waited for: 4 -> 2; matrix products, arithmetic and copies ran while one was open for 1% -> 2% of each run, Pallas kernels for 0% -> 0%
where the time goes in v6:
time: 157 us; the launch traced here: 156 us
  blocking collectives  109 us (69%)
  starting transfers between devices  24.4 us (16%)
  Pallas kernels  8.61 us (5%)
  waiting for transfers between devices  5.82 us (4%)
  other arithmetic  4.1 us (3%)
  between operations  2.14 us (1%)
  local copies, waits for them, and re-layouts  2.06 us (1%)
    unnamed x1, blocking collectives  41 us
    all_gather x1, blocking collectives, gather_scaled(): lax.all_gather(sent, ('zh', 'zl'), axis=0, tiled=True)  37.5 us
    all_to_all x2, blocking collectives, exchange(): return lax.all_to_all(value, axes, 0, 0, tiled=True)  30.5 us
    ppermute x2, starting transfers between devices, other_core(): return lax.ppermute(value, 'core', [(0, 1), (1, 0)])  20.3 us
    pallas_call x2, Pallas kernels, spmm(): pl.pallas_call(body, out_shape=jax.ShapeDtypeStruct(out_shape, jnp.bfloat...  6.95 us
    ppermute x1, waiting for transfers between devices, other_x(): return lax.ppermute(value, 'xl', [(0, 1), (1, 0)])  4.3 us
  transfers between devices with their start and end apart: 4, of which 2 were waited for; matrix products, arithmetic and copies ran while one was open for 2% of the time, Pallas kernels for 0%

profile of v6, /device:TPU:1, one launch (start us, length us, event | category | flops | bytes accessed | tf_op | source)
XLA Modules:
  0.0 156.1 jit_solution(10939264562407727512)
XLA Ops:
  0.6 0.7 multiply_multiply_fusion
  1.3 0.9 multiply_convert_fusion.1
  2.3 16.7 %all_to_all.10.rest_0_ = bf16[8,128,256]{2,1,0:T(8,128)(2,1)S(1)} all-to-all(bf16[8,128,256]{2,1,0:T(8,128)(2,1)S(1)} %broadcast_in_dim.6), channel_id=1, replica_groups=mesh['y'=4,'xh'=2,'core'=2,'zh'=8,'zl'=2,'xl'=2] {'y','xh'}, dimensions={0} | all-to-all | bytes 1048576 | tf_op jit(solution)/shard_map/all_to_all | solution.py:173
  18.9 5.0 %collective-permute-start = (bf16[8,128,256]{2,1,0:T(8,128)(2,1)S(1)}, bf16[8,128,256]{2,1,0:T(8,128)(2,1)S(1)}, u32[]{:S(2)}, u32[]{:S(2)}) collective-permute-start(bf16[8,128,256]{2,1,0:T(8,128)(2,1)S(1)} %all_to_all.10.rest_0_), channel_id=1, source_target_pairs={{0,32},{32,0},{1,33},{33,1},{2,34},{34,2},{3,35},{35,3},{4,36},{36... | collective-permute-start | bytes 1572872 | tf_op jit(solution)/shard_map/ppermute | solution.py:177
  24.0 0.7 convert_element_type.36
  25.3 0.7 add_bitcast_fusion
  26.0 0.0 collective-permute-done.rest_1_
  26.0 3.5 %shard_map.104 = bf16[4336,256]{1,0:T(8,128)(2,1)S(1)} custom-call(s32[1]{0:T(128)} %bitcast.16.count_ref, s32[96]{0:T(128)S(1)} %get-tuple-element.7.src_ref.dst_ref, s32[96]{0:T(128)S(1)} %get-tuple-element.6.dst_ref.src_ref, bf16[96,128,128]{2,1,0:T(8,128)(2,1)} %bitcast.21, bf16[8,128,256]{2,1,0:T(8,128)(2,1)S(1)} %all_to_all.10.rest_0_, ...), custom_call_target="tpu_custom_call" | custom-call | flops 805306368 | bytes 3145728 | tf_op jit(solution)/shard_map/pallas_call | solution.py:97
  29.5 0.0 copy-start
  29.5 0.0 copy-start.1
  29.5 0.0 copy-start.2
  29.6 41.0 %fusion = bf16[272,256]{1,0:T(8,128)(2,1)S(1)} fusion(bf16[4336,256]{1,0:T(8,128)(2,1)S(1)} %shard_map.104), kind=kCustom, calls=%all-reduce-scatter | all-reduce-scatter fusion | flops 1114113 | bytes 2361344
  70.6 1.9 %collective-permute-start.3 = (bf16[15,256]{1,0:T(8,128)(2,1)S(1)}, bf16[15,256]{1,0:T(8,128)(2,1)S(1)}, u32[]{:S(2)}, u32[]{:S(2)}) collective-permute-start(bf16[15,256]{1,0:T(8,128)(2,1)S(1)} %slice.20), channel_id=1, source_target_pairs={{0,2},{2,4},{4,6},{6,8},{8,10},{10,12},{12,14},{14,16},{16,18},{18... | collective-permute-start | bytes 23048
  72.6 1.3 dynamic-slice.4
  74.5 0.0 collective-permute-done.3
  74.5 0.5 concatenate.4
  75.1 0.0 copy-done
  75.1 2.2 %collective-permute-start.1 = (bf16[400,256]{1,0:T(8,128)(2,1)S(1)}, bf16[400,256]{1,0:T(8,128)(2,1)S(1)}, u32[]{:S(2)}, u32[]{:S(2)}) collective-permute-start(bf16[400,256]{1,0:T(8,128)(2,1)S(1)} %pad_maximum_fusion), channel_id=1, source_target_pairs={{0,1},{1,0},{2,3},{3,2},{4,5},{5,4},{6,7},{7,6},{8,9},{9,8},{10,11... | collective-permute-start | bytes 614408 | tf_op jit(solution)/shard_map/ppermute | solution.py:189
  77.3 4.3 %collective-permute-done.1.received_ref = bf16[400,256]{1,0:T(8,128)(2,1)S(1)} collective-permute-done((bf16[400,256]{1,0:T(8,128)(2,1)S(1)}, bf16[400,256]{1,0:T(8,128)(2,1)S(1)}, u32[]{:S(2)}, u32[]{:S(2)}) %collective-permute-start.1) | collective-permute-done | bytes 204832 | tf_op jit(solution)/shard_map/ppermute | solution.py:189
  81.6 0.0 copy-done.1
  81.6 0.0 copy-done.2
  81.6 0.9 shard_map.105
  82.6 37.5 %all-gather.1 = f16[4224,256]{1,0:T(8,128)(2,1)S(1)} all-gather(f16[264,256]{1,0:T(8,128)(2,1)S(1)} %convert_element_type.37), channel_id=1, replica_groups=mesh['y'=4,'xh'=2,'core'=2,'zh'=8,'zl'=2,'xl'=2] {'zh','zl'}, dimensions={0}, use_global_device_ids=true | all-gather | bytes 2297856 | tf_op jit(solution)/shard_map/all_gather | solution.py:182
  120.1 0.1 copy.13
  120.2 1.0 multiply_convert_fusion
  121.2 3.4 %shard_map.106 = bf16[16,128,256]{2,1,0:T(8,128)(2,1)S(1)} custom-call(s32[1]{0:T(128)} %bitcast.17.count_ref, s32[96]{0:T(128)S(1)} %get-tuple-element.6.dst_ref.src_ref, s32[96]{0:T(128)S(1)} %get-tuple-element.7.src_ref.dst_ref, bf16[96,128,128]{2,1,0:T(8,128)(2,1)} %bitcast.22, bf16[32,128,256]{2,1,0:T(8,128)(2,1)S(1)} %bitcast.18), custom_call_target="tpu_custom_call" | custom-call | flops 805306368 | bytes 3145728 | tf_op jit(solution)/shard_map/pallas_call | solution.py:97
  124.7 15.2 %collective-permute-start.2 = (bf16[8,128,256]{2,1,0:T(8,128)(2,1)S(1)}, bf16[8,128,256]{2,1,0:T(8,128)(2,1)S(1)}, u32[]{:S(2)}, u32[]{:S(2)}) collective-permute-start(bf16[8,128,256]{2,1,0:T(8,128)(2,1)S(1)} %slice.19), channel_id=1, source_target_pairs={{0,32},{32,0},{1,33},{33,1},{2,34},{34,2},{3,35},{35,3},{4,36},{36... | collective-permute-start | bytes 1572872 | tf_op jit(solution)/shard_map/ppermute | solution.py:177
  139.9 1.5 collective-permute-done.2
  141.4 0.1 add_convert_fusion
  141.6 13.9 %all_to_all.11.parts_ref = bf16[8,128,256]{2,1,0:T(8,128)(2,1)S(1)} all-to-all(bf16[8,128,256]{2,1,0:T(8,128)(2,1)S(1)} %add_convert_fusion), channel_id=1, replica_groups=mesh['y'=4,'xh'=2,'core'=2,'zh'=8,'zl'=2,'xl'=2] {'y','xh'}, dimensions={0} | all-to-all | bytes 1048576 | tf_op jit(solution)/shard_map/all_to_all | solution.py:173
  155.4 0.7 shard_map.107
  (11 shorter events, 0.2 us)
Async XLA Ops:
  18.9 7.1 %collective-permute-start = (bf16[8,128,256]{2,1,0:T(8,128)(2,1)S(1)}, bf16[8,128,256]{2,1,0:T(8,128)(2,1)S(1)}, u32[]{:S(2)}, u32[]{:S(2)}) collective-permute-start(bf16[8,128,256]{2,1,0:T(8,128)(2,1)S(1)} %all_to_all.10.rest_0_), channel_id=1, source_target_pairs={{0,32},{32,0},{1,33},{33,1},{2,34},{34,2},{3,35},{35,3},{4,36},{36... | collective-permute-start | bytes 1572872 | tf_op jit(solution)/shard_map/ppermute | solution.py:177
  29.5 45.6 %copy-start = (bf16[128,256]{1,0:T(8,128)(2,1)S(1)}, bf16[128,256]{1,0:T(8,128)(2,1)}, u32[]{:S(2)}) copy-start(bf16[128,256]{1,0:T(8,128)(2,1)} %cotangent_ref.1) | copy-start | bytes 196612
  29.5 52.1 %copy-start.1 = (bf16[256,256]{1,0:T(8,128)(2,1)S(1)}, bf16[256,256]{1,0:T(8,128)(2,1)}, u32[]{:S(2)}) copy-start(bf16[256,256]{1,0:T(8,128)(2,1)} %weight_ref.1) | copy-start | bytes 393220
  29.5 52.1 %copy-start.2 = (s32[128]{0:T(128)S(1)}, s32[128]{0:T(128)}, u32[]{:S(2)}) copy-start(s32[128]{0:T(128)} %param.11) | copy-start | bytes 1540
  70.6 3.9 %collective-permute-start.3 = (bf16[15,256]{1,0:T(8,128)(2,1)S(1)}, bf16[15,256]{1,0:T(8,128)(2,1)S(1)}, u32[]{:S(2)}, u32[]{:S(2)}) collective-permute-start(bf16[15,256]{1,0:T(8,128)(2,1)S(1)} %slice.20), channel_id=1, source_target_pairs={{0,2},{2,4},{4,6},{6,8},{8,10},{10,12},{12,14},{14,16},{16,18},{18... | collective-permute-start | bytes 23048
  75.1 6.5 %collective-permute-start.1 = (bf16[400,256]{1,0:T(8,128)(2,1)S(1)}, bf16[400,256]{1,0:T(8,128)(2,1)S(1)}, u32[]{:S(2)}, u32[]{:S(2)}) collective-permute-start(bf16[400,256]{1,0:T(8,128)(2,1)S(1)} %pad_maximum_fusion), channel_id=1, source_target_pairs={{0,1},{1,0},{2,3},{3,2},{4,5},{5,4},{6,7},{7,6},{8,9},{9,8},{10,11... | collective-permute-start | bytes 614408 | tf_op jit(solution)/shard_map/ppermute | solution.py:189
  124.7 16.7 %collective-permute-start.2 = (bf16[8,128,256]{2,1,0:T(8,128)(2,1)S(1)}, bf16[8,128,256]{2,1,0:T(8,128)(2,1)S(1)}, u32[]{:S(2)}, u32[]{:S(2)}) collective-permute-start(bf16[8,128,256]{2,1,0:T(8,128)(2,1)S(1)} %slice.19), channel_id=1, source_target_pairs={{0,32},{32,0},{1,33},{33,1},{2,34},{34,2},{3,35},{35,3},{4,36},{36... | collective-permute-start | bytes 1572872 | tf_op jit(solution)/shard_map/ppermute | solution.py:177

commit v7 on v6

--- a/solution.py
+++ b/solution.py
@@ -10,9 +10,9 @@
 HID = 256
 BSZ = 128
 QDEN = 192
-GROUP = 32
+GROUP = 48
 AHEAD = 1
-CHUNK = 32
+CHUNK = 48
 SPREAD = 2 * BSZ + 16
 
 NAMES = ("y", "xh", "core", "zh", "zl", "xl")

time: 157 us -> 158 us (level)
  blocking collectives: 109 us -> 111 us
where the time goes in v7:
time: 158 us; the launch traced here: 157 us
  blocking collectives  111 us (70%)
  starting transfers between devices  23.7 us (15%)
  Pallas kernels  8.04 us (5%)
  waiting for transfers between devices  6.09 us (4%)
  other arithmetic  4.1 us (3%)
  between operations  2.14 us (1%)
  local copies, waits for them, and re-layouts  2.06 us (1%)
    unnamed x1, blocking collectives  41.8 us
    all_gather x1, blocking collectives, gather_scaled(): lax.all_gather(sent, ('zh', 'zl'), axis=0, tiled=True)  38.1 us
    all_to_all x2, blocking collectives, exchange(): return lax.all_to_all(value, axes, 0, 0, tiled=True)  31.4 us
    ppermute x2, starting transfers between devices, other_core(): return lax.ppermute(value, 'core', [(0, 1), (1, 0)])  19.8 us
    pallas_call x2, Pallas kernels, spmm(): pl.pallas_call(body, out_shape=jax.ShapeDtypeStruct(out_shape, jnp.bfloat...  6.37 us
    ppermute x1, waiting for transfers between devices, other_x(): return lax.ppermute(value, 'xl', [(0, 1), (1, 0)])  4.57 us
  transfers between devices with their start and end apart: 4, of which 2 were waited for; matrix products, arithmetic and copies ran while one was open for 2% of the time, Pallas kernels for 0%

profile of v7, /device:TPU:1, one launch (start us, length us, event | category | flops | bytes accessed | tf_op | source)
XLA Modules:
  0.0 157.4 jit_solution(14437812059635554655)
XLA Ops:
  0.6 0.7 multiply_multiply_fusion
  1.3 0.9 multiply_convert_fusion.1
  2.3 16.7 %all_to_all.10.rest_0_ = bf16[8,128,256]{2,1,0:T(8,128)(2,1)S(1)} all-to-all(bf16[8,128,256]{2,1,0:T(8,128)(2,1)S(1)} %broadcast_in_dim.6), channel_id=1, replica_groups=mesh['y'=4,'xh'=2,'core'=2,'zh'=8,'zl'=2,'xl'=2] {'y','xh'}, dimensions={0} | all-to-all | bytes 1048576 | tf_op jit(solution)/shard_map/all_to_all | solution.py:173
  18.9 5.0 %collective-permute-start = (bf16[8,128,256]{2,1,0:T(8,128)(2,1)S(1)}, bf16[8,128,256]{2,1,0:T(8,128)(2,1)S(1)}, u32[]{:S(2)}, u32[]{:S(2)}) collective-permute-start(bf16[8,128,256]{2,1,0:T(8,128)(2,1)S(1)} %all_to_all.10.rest_0_), channel_id=1, source_target_pairs={{0,32},{32,0},{1,33},{33,1},{2,34},{34,2},{3,35},{35,3},{4,36},{36... | collective-permute-start | bytes 1572872 | tf_op jit(solution)/shard_map/ppermute | solution.py:177
  24.0 0.7 convert_element_type.36
  25.3 0.7 add_bitcast_fusion
  26.0 0.0 collective-permute-done.rest_1_
  26.0 3.2 %shard_map.104 = bf16[4336,256]{1,0:T(8,128)(2,1)S(1)} custom-call(s32[1]{0:T(128)} %bitcast.16.count_ref, s32[96]{0:T(128)S(1)} %get-tuple-element.7.src_ref.dst_ref, s32[96]{0:T(128)S(1)} %get-tuple-element.6.dst_ref.src_ref, bf16[96,128,128]{2,1,0:T(8,128)(2,1)} %bitcast.21, bf16[8,128,256]{2,1,0:T(8,128)(2,1)S(1)} %all_to_all.10.rest_0_, ...), custom_call_target="tpu_custom_call" | custom-call | flops 805306368 | bytes 3145728 | tf_op jit(solution)/shard_map/pallas_call | solution.py:97
  29.2 0.0 copy-start
  29.2 0.0 copy-start.1
  29.2 0.0 copy-start.2
  29.2 41.8 %fusion = bf16[272,256]{1,0:T(8,128)(2,1)S(1)} fusion(bf16[4336,256]{1,0:T(8,128)(2,1)S(1)} %shard_map.104), kind=kCustom, calls=%all-reduce-scatter | all-reduce-scatter fusion | flops 1114113 | bytes 2361344
  71.0 2.0 %collective-permute-start.3 = (bf16[15,256]{1,0:T(8,128)(2,1)S(1)}, bf16[15,256]{1,0:T(8,128)(2,1)S(1)}, u32[]{:S(2)}, u32[]{:S(2)}) collective-permute-start(bf16[15,256]{1,0:T(8,128)(2,1)S(1)} %slice.20), channel_id=1, source_target_pairs={{0,2},{2,4},{4,6},{6,8},{8,10},{10,12},{12,14},{14,16},{16,18},{18... | collective-permute-start | bytes 23048
  73.1 1.3 dynamic-slice.4
  75.0 0.0 collective-permute-done.3
  75.0 0.5 concatenate.4
  75.6 0.0 copy-done
  75.7 1.9 %collective-permute-start.1 = (bf16[400,256]{1,0:T(8,128)(2,1)S(1)}, bf16[400,256]{1,0:T(8,128)(2,1)S(1)}, u32[]{:S(2)}, u32[]{:S(2)}) collective-permute-start(bf16[400,256]{1,0:T(8,128)(2,1)S(1)} %pad_maximum_fusion), channel_id=1, source_target_pairs={{0,1},{1,0},{2,3},{3,2},{4,5},{5,4},{6,7},{7,6},{8,9},{9,8},{10,11... | collective-permute-start | bytes 614408 | tf_op jit(solution)/shard_map/ppermute | solution.py:189
  77.6 4.6 %collective-permute-done.1.received_ref = bf16[400,256]{1,0:T(8,128)(2,1)S(1)} collective-permute-done((bf16[400,256]{1,0:T(8,128)(2,1)S(1)}, bf16[400,256]{1,0:T(8,128)(2,1)S(1)}, u32[]{:S(2)}, u32[]{:S(2)}) %collective-permute-start.1) | collective-permute-done | bytes 204832 | tf_op jit(solution)/shard_map/ppermute | solution.py:189
  82.2 0.0 copy-done.1
  82.2 0.0 copy-done.2
  82.2 0.9 shard_map.105
  83.1 38.1 %all-gather.1 = f16[4224,256]{1,0:T(8,128)(2,1)S(1)} all-gather(f16[264,256]{1,0:T(8,128)(2,1)S(1)} %convert_element_type.37), channel_id=1, replica_groups=mesh['y'=4,'xh'=2,'core'=2,'zh'=8,'zl'=2,'xl'=2] {'zh','zl'}, dimensions={0}, use_global_device_ids=true | all-gather | bytes 2297856 | tf_op jit(solution)/shard_map/all_gather | solution.py:182
  121.3 0.1 copy.13
  121.4 1.0 multiply_convert_fusion
  122.3 3.2 %shard_map.106 = bf16[16,128,256]{2,1,0:T(8,128)(2,1)S(1)} custom-call(s32[1]{0:T(128)} %bitcast.17.count_ref, s32[96]{0:T(128)S(1)} %get-tuple-element.6.dst_ref.src_ref, s32[96]{0:T(128)S(1)} %get-tuple-element.7.src_ref.dst_ref, bf16[96,128,128]{2,1,0:T(8,128)(2,1)} %bitcast.22, bf16[32,128,256]{2,1,0:T(8,128)(2,1)S(1)} %bitcast.18), custom_call_target="tpu_custom_call" | custom-call | flops 805306368 | bytes 3145728 | tf_op jit(solution)/shard_map/pallas_call | solution.py:97
  125.6 14.7 %collective-permute-start.2 = (bf16[8,128,256]{2,1,0:T(8,128)(2,1)S(1)}, bf16[8,128,256]{2,1,0:T(8,128)(2,1)S(1)}, u32[]{:S(2)}, u32[]{:S(2)}) collective-permute-start(bf16[8,128,256]{2,1,0:T(8,128)(2,1)S(1)} %slice.19), channel_id=1, source_target_pairs={{0,32},{32,0},{1,33},{33,1},{2,34},{34,2},{3,35},{35,3},{4,36},{36... | collective-permute-start | bytes 1572872 | tf_op jit(solution)/shard_map/ppermute | solution.py:177
  140.3 1.5 collective-permute-done.2
  141.8 0.1 add_convert_fusion
  142.0 14.7 %all_to_all.11.parts_ref = bf16[8,128,256]{2,1,0:T(8,128)(2,1)S(1)} all-to-all(bf16[8,128,256]{2,1,0:T(8,128)(2,1)S(1)} %add_convert_fusion), channel_id=1, replica_groups=mesh['y'=4,'xh'=2,'core'=2,'zh'=8,'zl'=2,'xl'=2] {'y','xh'}, dimensions={0} | all-to-all | bytes 1048576 | tf_op jit(solution)/shard_map/all_to_all | solution.py:173
  156.7 0.7 shard_map.107
  (11 shorter events, 0.2 us)
Async XLA Ops:
  18.9 7.1 %collective-permute-start = (bf16[8,128,256]{2,1,0:T(8,128)(2,1)S(1)}, bf16[8,128,256]{2,1,0:T(8,128)(2,1)S(1)}, u32[]{:S(2)}, u32[]{:S(2)}) collective-permute-start(bf16[8,128,256]{2,1,0:T(8,128)(2,1)S(1)} %all_to_all.10.rest_0_), channel_id=1, source_target_pairs={{0,32},{32,0},{1,33},{33,1},{2,34},{34,2},{3,35},{35,3},{4,36},{36... | collective-permute-start | bytes 1572872 | tf_op jit(solution)/shard_map/ppermute | solution.py:177
  29.2 46.4 %copy-start = (bf16[128,256]{1,0:T(8,128)(2,1)S(1)}, bf16[128,256]{1,0:T(8,128)(2,1)}, u32[]{:S(2)}) copy-start(bf16[128,256]{1,0:T(8,128)(2,1)} %cotangent_ref.1) | copy-start | bytes 196612
  29.2 52.9 %copy-start.1 = (bf16[256,256]{1,0:T(8,128)(2,1)S(1)}, bf16[256,256]{1,0:T(8,128)(2,1)}, u32[]{:S(2)}) copy-start(bf16[256,256]{1,0:T(8,128)(2,1)} %weight_ref.1) | copy-start | bytes 393220
  29.2 52.9 %copy-start.2 = (s32[128]{0:T(128)S(1)}, s32[128]{0:T(128)}, u32[]{:S(2)}) copy-start(s32[128]{0:T(128)} %param.11) | copy-start | bytes 1540
  71.0 4.0 %collective-permute-start.3 = (bf16[15,256]{1,0:T(8,128)(2,1)S(1)}, bf16[15,256]{1,0:T(8,128)(2,1)S(1)}, u32[]{:S(2)}, u32[]{:S(2)}) collective-permute-start(bf16[15,256]{1,0:T(8,128)(2,1)S(1)} %slice.20), channel_id=1, source_target_pairs={{0,2},{2,4},{4,6},{6,8},{8,10},{10,12},{12,14},{14,16},{16,18},{18... | collective-permute-start | bytes 23048
  75.7 6.5 %collective-permute-start.1 = (bf16[400,256]{1,0:T(8,128)(2,1)S(1)}, bf16[400,256]{1,0:T(8,128)(2,1)S(1)}, u32[]{:S(2)}, u32[]{:S(2)}) collective-permute-start(bf16[400,256]{1,0:T(8,128)(2,1)S(1)} %pad_maximum_fusion), channel_id=1, source_target_pairs={{0,1},{1,0},{2,3},{3,2},{4,5},{5,4},{6,7},{7,6},{8,9},{9,8},{10,11... | collective-permute-start | bytes 614408 | tf_op jit(solution)/shard_map/ppermute | solution.py:189
  125.6 16.3 %collective-permute-start.2 = (bf16[8,128,256]{2,1,0:T(8,128)(2,1)S(1)}, bf16[8,128,256]{2,1,0:T(8,128)(2,1)S(1)}, u32[]{:S(2)}, u32[]{:S(2)}) collective-permute-start(bf16[8,128,256]{2,1,0:T(8,128)(2,1)S(1)} %slice.19), channel_id=1, source_target_pairs={{0,32},{32,0},{1,33},{33,1},{2,34},{34,2},{3,35},{35,3},{4,36},{36... | collective-permute-start | bytes 1572872 | tf_op jit(solution)/shard_map/ppermute | solution.py:177
